TPU v7x, 32 devices: a whole 2x2x4 slice. The times are simulated.
32 devices in a mesh: pair: 4 (over z), blk: 8 (over y, x, core).
Axes of the slice: x: 2, y: 2, z: 4, core: 2. Of those that a mesh axis runs over, the one named last changes fastest.
Arguments:
- spectra: bfloat16 [3000, 4096], P(None, ('pair', 'blk')), may hold values from -24 to 24
- wedge_ids: int32 [2048], P(('pair', 'blk')), may hold values from 0 to 7
- tilt_limits: int32 [8, 2], replicated, may hold values from 4 to 15
- term_freqs: int32 [3, 3000], replicated, may hold values from -12 to 11, as said below
Outputs:
- best_match: float32 [2048, 256], P(('pair', 'blk'))
Inputs may be any that keep to these rules, and one draw needn't show every extreme that they name: `term_freqs`: each entry is a frequency index along one axis of the 24-cell box.
All inputs are finite; a program needn't handle non-finite values.
Results may differ from a plain program's by a relative error of at most 0.00065.
Values may be sent and summed in bfloat16 or wider, within the bound.
No kernel may reach another device: no remote copies, remote signals or barrier semaphores. Data moves between devices by JAX's collectives and lax.ppermute only.
A program may use at most 64 MiB of HBM per device.

v0:
```python
import math

import jax
import jax.numpy as jnp
from jax import lax
from jax.sharding import PartitionSpec as P

BOX = 24
RADIUS = 1
SHIFTS = 27
STEPS = 2
ROUND = 2


epsilon = 1e-06


def partner_2(value, axis, distance):
    mask = 2**distance
    pairs = [(source, source ^ mask) for source in range(lax.axis_size(axis))]
    return lax.ppermute(value, axis, pairs)


def from_behind(block, axis, distance):
    devices = range(lax.axis_size(axis))
    route = [((i - distance) % len(devices), i) for i in devices]
    return lax.ppermute(block, axis, route)


def wedge_table(term_freqs, tilt_limits):
    first_axis = term_freqs[0][:, None]
    third_axis = term_freqs[2][:, None]
    limit_value = jnp.where(
        first_axis * third_axis >= 0, tilt_limits[:, 0][None, :], tilt_limits[:, 1][None, :]
    )
    measured = 4 * third_axis * third_axis <= limit_value * first_axis * first_axis
    return jnp.where(measured, 1.0, 0.0).astype(jnp.float32)


def shift_phases(term_freqs):
    span_cells = 2 * RADIUS + 1
    shift_index = jnp.arange(SHIFTS, dtype=jnp.int32)
    offset_first = shift_index // (span_cells * span_cells) - RADIUS
    offset_second = shift_index // span_cells % span_cells - RADIUS
    offset_third = shift_index % span_cells - RADIUS
    phase_turns = (
        offset_first[:, None] * term_freqs[0][None, :]
        + offset_second[:, None] * term_freqs[1][None, :]
        + offset_third[:, None] * term_freqs[2][None, :]
    )
    phase_angle = phase_turns.astype(jnp.float32) * (2.0 * math.pi / BOX)
    return (jnp.cos(phase_angle), jnp.sin(phase_angle))


def class_choice(class_count, wedge_ids, dtype):
    classes = jnp.arange(class_count, dtype=jnp.int32)
    return (classes[:, None] == wedge_ids[None, :]).astype(dtype)


def mask_block(spectra, wedge_ids, table):
    both_ids = jnp.concatenate([wedge_ids, wedge_ids], axis=0)
    chosen = class_choice(table.shape[1], both_ids, jnp.bfloat16)
    measured = jnp.dot(table.astype(jnp.bfloat16), chosen, preferred_element_type=jnp.float32)
    return spectra * measured.astype(jnp.bfloat16)


def class_powers(packed, table):
    half_width = packed.shape[1] // 2
    squared = jnp.square(packed.astype(jnp.float32))
    power_terms = squared[:, :half_width] + squared[:, half_width:]
    return lax.dot_general(
        power_terms,
        table,
        (((0,), (0,)), ((), ())),
        precision=lax.Precision.HIGHEST,
        preferred_element_type=jnp.float32,
    )


def pick_columns(values, wedge_ids):
    chosen = class_choice(values.shape[1], wedge_ids, jnp.float32)
    return jnp.dot(
        values, chosen, precision=lax.Precision.HIGHEST, preferred_element_type=jnp.float32
    )


def across_groups(payload):
    for bit_index in range(lax.axis_size("pair").bit_length() - 1):
        if ROUND >> bit_index & 1:
            payload = partner_2((payload[0], payload[1]), "pair", bit_index)
    return payload


def tiles_across(payload):
    for bit_index in range(lax.axis_size("pair").bit_length() - 1):
        if ROUND >> bit_index & 1:
            payload = partner_2(payload, "pair", bit_index)
    return payload


def reach_blocks(payload):
    gathered = []
    current = payload
    for offset in range(1, STEPS + 1):
        current = from_behind((current[0], current[1]), "blk", -1)
        gathered.append(current)
    return gathered


def shards(spectra, wedge_ids, tilt_limits, term_freqs):
    row_count = wedge_ids.shape[0]
    table = wedge_table(term_freqs, tilt_limits)
    cosine_table, sine_table = shift_phases(term_freqs)
    masked = mask_block(spectra, wedge_ids, table)
    own_power = class_powers(masked, table)
    partner = across_groups((masked, wedge_ids))
    fetched = reach_blocks(partner)
    column_real = jnp.concatenate([entry[0][:, :row_count] for entry in fetched], axis=1)
    column_imag = jnp.concatenate([entry[0][:, row_count:] for entry in fetched], axis=1)
    column_both = jnp.concatenate([column_real, column_imag], axis=0)
    column_ids = jnp.concatenate([entry[1] for entry in fetched], axis=0)
    column_power = jnp.concatenate([class_powers(entry[0], table) for entry in fetched], axis=0)
    real_part = masked[:, :row_count].astype(jnp.float32)
    imag_part = masked[:, row_count:].astype(jnp.float32)
    term_count = real_part.shape[0]
    column_count = column_both.shape[1]
    group_size = 2 * RADIUS + 1
    contract = (((0,), (0,)), ((), ()))

    def one_group(group_index, running):
        first_shift = group_index * group_size
        cosine_rows = lax.dynamic_slice_in_dim(cosine_table, first_shift, group_size, 0)[:, :, None]
        sine_rows = lax.dynamic_slice_in_dim(sine_table, first_shift, group_size, 0)[:, :, None]
        rotated_real = real_part[None] * cosine_rows + imag_part[None] * sine_rows
        rotated_imag = imag_part[None] * cosine_rows - real_part[None] * sine_rows
        rotated = jnp.concatenate([rotated_real, rotated_imag], axis=1)
        rotated = jnp.transpose(rotated, (1, 0, 2)).reshape(2 * term_count, group_size * row_count)
        rotated_high = rotated.astype(jnp.bfloat16)
        rotated_low = (rotated - rotated_high.astype(jnp.float32)).astype(jnp.bfloat16)
        scores = lax.dot_general(
            rotated_high, column_both, contract, preferred_element_type=jnp.float32
        )
        scores = scores + lax.dot_general(
            rotated_low, column_both, contract, preferred_element_type=jnp.float32
        )
        scores = scores.reshape(group_size, row_count, column_count)
        return jnp.maximum(running, jnp.max(scores, axis=0))

    starting = jnp.full((row_count, column_count), -jnp.inf, jnp.float32)
    largest = lax.fori_loop(0, SHIFTS // group_size, one_group, starting)
    row_norm = pick_columns(own_power, column_ids)
    column_norm = pick_columns(column_power, wedge_ids).T
    local_best = largest * lax.rsqrt(row_norm * column_norm + epsilon)
    returned_tiles = tiles_across(local_best)
    backward = []
    for offset in range(1, STEPS + 1):
        tile_slice = returned_tiles[:, (offset - 1) * row_count : offset * row_count]
        arrived = from_behind(tile_slice, "blk", offset)
        backward.append(arrived.T)
    return jnp.concatenate([local_best] + backward, axis=1)


def solution(mesh):
    placed = (P(None, ("pair", "blk")), P(("pair", "blk")), P(), P())
    return jax.shard_map(
        shards, mesh=mesh, in_specs=placed, out_specs=P(("pair", "blk"), None), check_vma=False
    )
```

profile of v0, /device:TPU:0, one launch (start us, length us, event | category | flops | bytes accessed | tf_op | source)
XLA Modules:
  0.0 125.9 jit_solution(14177712881954971430)
XLA Ops:
  0.0 4.0 %collective-permute-start.3 = (s32[64]{0:T(128)}, s32[64]{0:T(128)S(1)}, u32[]{:S(2)}, u32[]{:S(2)}) collective-permute-start(s32[64]{0:T(128)} %param.7), channel_id=1, source_target_pairs={{0,16},{8,24},{16,0},{24,8},{1,17},{9,25},{17,1},{25,9},{2,18},{10... | collective-permute-start | bytes 776 | tf_op jit(solution)/shard_map/ppermute | solution.py:21
  4.0 0.8 pad_add_fusion
  4.8 0.8 slice_bitcast_fusion.1
  5.6 0.9 fusion.46
  6.6 1.8 %convert_multiply_fusion.2 = (f32[3000,128]{1,0:T(8,128)S(1)}, bf16[3000,128]{1,0:T(8,128)(2,1)S(1)}) fusion(bf16[3000,128]{1,0:T(8,128)(2,1)} %param.6, s32[128]{0:T(128)S(1)} %pad_add_fusion, s32[3000]{0:T(1024)S(1)} %bitcast.37, s32[8]{0:T(128)S(1)} %get-tuple-element.209, s32[8]{0:T(128)S(1)} %get-tuple-element.208, ...), kind=kOutput, calls=%fused_computation.24 | convolution fusion | flops 7825024 | bytes 3099576 | tf_op jit(solution)/shard_map/dot_general | solution.py:63
  8.5 1.9 %slice_convert_fusion = (f32[3000,64]{1,0:T(8,128)}, f32[3000,64]{1,0:T(8,128)}) fusion(bf16[3000,128]{1,0:T(8,128)(2,1)S(1)} %get-tuple-element.211), kind=kLoop, calls=%fused_computation.28 | loop fusion | flops 384000 | bytes 2304000 | tf_op jit(solution)/shard_map/convert_element_type | solution.py:124
  10.4 34.0 %collective-permute-done = bf16[3000,128]{1,0:T(8,128)(2,1)S(1)} collective-permute-done((bf16[3000,128]{1,0:T(8,128)(2,1)S(1)}, bf16[3000,128]{1,0:T(8,128)(2,1)S(1)}, u32[]{:S(2)}, u32[]{:S(2)}) %collective-permute-start) | collective-permute-done | bytes 768032 | tf_op jit(solution)/shard_map/ppermute | solution.py:21
  44.4 1.0 collective-permute-start.1
  45.4 2.4 %fusion.10 = (f32[27,3000]{1,0:T(8,128)}, f32[27,3000]{1,0:T(8,128)}) fusion(s32[3000]{0:T(1024)S(1)} %bitcast.44, s32[27]{0:T(128)S(1)} %get-tuple-element.213, s32[3000]{0:T(1024)S(1)} %bitcast.45, s32[27]{0:T(128)S(1)} %get-tuple-element.212, s32[3000]{0:T(1024)S(1)} %bitcast.38, s32[27]{0:T(128)S(1)} %fusion.33), kind=kLoop, calls=%fused_computation.31 | loop fusion | flops 567000 | bytes 684324 | tf_op jit(solution)/shard_map/sin | solution.py:52
  47.8 1.6 %collective-permute-start.4 = (s32[64]{0:T(128)S(1)}, s32[64]{0:T(128)S(1)}, u32[]{:S(2)}, u32[]{:S(2)}) collective-permute-start(s32[64]{0:T(128)S(1)} %collective-permute-done.3), channel_id=1, source_target_pairs={{1,0},{2,1},{3,2},{4,3},{5,4},{6,5},{7,6},{0,7},{9,8},{10,9},{11,1... | collective-permute-start | bytes 776 | tf_op jit(solution)/shard_map/ppermute | solution.py:27
  49.4 1.1 fusion.6
  50.5 4.3 %collective-permute-done.4 = s32[64]{0:T(128)S(1)} collective-permute-done((s32[64]{0:T(128)S(1)}, s32[64]{0:T(128)S(1)}, u32[]{:S(2)}, u32[]{:S(2)}) %collective-permute-start.4) | collective-permute-done | bytes 288 | tf_op jit(solution)/shard_map/ppermute | solution.py:27
  54.8 2.8 %collective-permute-start.5 = (s32[64]{0:T(128)S(1)}, s32[64]{0:T(128)S(1)}, u32[]{:S(2)}, u32[]{:S(2)}) collective-permute-start(s32[64]{0:T(128)S(1)} %collective-permute-done.4), channel_id=1, source_target_pairs={{1,0},{2,1},{3,2},{4,3},{5,4},{6,5},{7,6},{0,7},{9,8},{10,9},{11,1... | collective-permute-start | bytes 776 | tf_op jit(solution)/shard_map/ppermute | solution.py:27
  57.6 1.8 %copy.13 = f32[3000,64]{0,1:T(8,128)S(1)} copy(f32[3000,64]{1,0:T(8,128)} %get-tuple-element.199) | data formatting | bytes 1536000
  59.4 1.8 %copy.12 = f32[3000,64]{0,1:T(8,128)S(1)} copy(f32[3000,64]{1,0:T(8,128)} %get-tuple-element.200) | data formatting | bytes 1536000
  61.6 1.1 fusion.4
  63.1 7.8 %collective-permute-done.2 = bf16[3000,128]{1,0:T(8,128)(2,1)S(1)} collective-permute-done((bf16[3000,128]{1,0:T(8,128)(2,1)S(1)}, bf16[3000,128]{1,0:T(8,128)(2,1)S(1)}, u32[]{:S(2)}, u32[]{:S(2)}) %collective-permute-start.2) | collective-permute-done | bytes 768032 | tf_op jit(solution)/shard_map/ppermute | solution.py:27
  71.0 1.1 fusion.2
  72.4 0.8 maximum_maximum_fusion
  73.2 41.0 %while.14 = (s32[]{:T(128)}, f32[64,128]{1,0:T(8,128)S(1)}, f32[3000,64]{0,1:T(8,128)S(1)}, f32[27,3000]{1,0:T(8,128)}, f32[3000,64]{0,1:T(8,128)S(1)}, /*index=...) while((s32[]{:T(128)}, f32[64,128]{1,0:T(8,128)S(1)}, ...), condition=%wide.region_2.3_spmd.clone, body=%wide.region_0.2_spmd.clone.sunk | while | flops 599097344 | bytes 32996476 | solution.py:150
  73.3 1.1 constant_dynamic-slice_fusion.3
  74.3 0.7 multiply_add_fusion.2
  75.0 0.8 pad_maximum_fusion.3
  76.1 0.8 fusion.65
  77.0 0.8 convolution_add_fusion.2
  77.8 1.1 constant_dynamic-slice_fusion.3
  78.9 0.7 multiply_add_fusion.2
  79.5 0.8 pad_maximum_fusion.3
  80.7 0.8 fusion.65
  81.5 0.8 convolution_add_fusion.2
  82.4 1.1 constant_dynamic-slice_fusion.3
  83.4 0.7 multiply_add_fusion.2
  84.1 0.8 pad_maximum_fusion.3
  85.3 0.8 fusion.65
  86.1 0.8 convolution_add_fusion.2
  86.9 1.1 constant_dynamic-slice_fusion.3
  88.7 0.8 pad_maximum_fusion.3
  89.8 0.8 fusion.65
  90.6 0.8 convolution_add_fusion.2
  91.5 1.1 constant_dynamic-slice_fusion.3
  93.2 0.8 pad_maximum_fusion.3
  94.4 0.8 fusion.65
  95.2 0.8 convolution_add_fusion.2
  96.1 1.1 constant_dynamic-slice_fusion.3
  97.8 0.8 pad_maximum_fusion.3
  99.0 0.8 fusion.65
  99.8 0.8 convolution_add_fusion.2
  100.6 1.1 constant_dynamic-slice_fusion.3
  102.3 0.8 pad_maximum_fusion.3
  103.5 0.8 fusion.65
  104.3 0.8 convolution_add_fusion.2
  105.2 1.1 constant_dynamic-slice_fusion.3
  106.9 0.8 pad_maximum_fusion.3
  108.1 0.8 fusion.65
  108.9 0.8 convolution_add_fusion.2
  109.7 1.0 constant_dynamic-slice_fusion.3
  111.4 0.8 pad_maximum_fusion.3
  112.5 0.8 fusion.65
  113.4 0.8 convolution_add_fusion.2
  114.9 5.4 %collective-permute-done.6 = f32[64,128]{0,1:T(8,128)S(1)} collective-permute-done((f32[64,128]{0,1:T(8,128)S(1)}, f32[64,128]{0,1:T(8,128)S(1)}, u32[]{:S(2)}, u32[]{:S(2)}) %collective-permute-start.6) | collective-permute-done | bytes 32800 | tf_op jit(solution)/shard_map/ppermute | solution.py:21
  120.3 1.2 collective-permute-start.8
  121.5 3.0 %collective-permute-done.7 = f32[64,64]{0,1:T(8,128)S(1)} collective-permute-done((f32[64,64]{0,1:T(8,128)S(1)}, f32[64,64]{0,1:T(8,128)S(1)}, u32[]{:S(2)}, u32[]{:S(2)}) %collective-permute-start.7) | collective-permute-done | bytes 16416 | tf_op jit(solution)/shard_map/ppermute | solution.py:27
  124.5 0.7 collective-permute-done.8
  125.2 0.7 pad_maximum_fusion.1
  (56 shorter events, 9.3 us)
Async XLA Ops:
  0.0 47.8 %collective-permute-start.3 = (s32[64]{0:T(128)}, s32[64]{0:T(128)S(1)}, u32[]{:S(2)}, u32[]{:S(2)}) collective-permute-start(s32[64]{0:T(128)} %param.7), channel_id=1, source_target_pairs={{0,16},{8,24},{16,0},{24,8},{1,17},{9,25},{17,1},{25,9},{2,18},{10... | collective-permute-start | bytes 776 | tf_op jit(solution)/shard_map/ppermute | solution.py:21
  8.4 36.0 %collective-permute-start = (bf16[3000,128]{1,0:T(8,128)(2,1)S(1)}, bf16[3000,128]{1,0:T(8,128)(2,1)S(1)}, u32[]{:S(2)}, u32[]{:S(2)}) collective-permute-start(bf16[3000,128]{1,0:T(8,128)(2,1)S(1)} %get-tuple-element.211), channel_id=1, source_target_pairs={{0,16},{8,24},{16,0},{24,8},{1,17},{9,25},{17,1},{25,9},{2,18},{10... | collective-permute-start | bytes 2304008 | tf_op jit(solution)/shard_map/ppermute | solution.py:21
  44.4 17.0 %collective-permute-start.1 = (bf16[3000,128]{1,0:T(8,128)(2,1)S(1)}, bf16[3000,128]{1,0:T(8,128)(2,1)S(1)}, u32[]{:S(2)}, u32[]{:S(2)}) collective-permute-start(bf16[3000,128]{1,0:T(8,128)(2,1)S(1)} %collective-permute-done), channel_id=1, source_target_pairs={{1,0},{2,1},{3,2},{4,3},{5,4},{6,5},{7,6},{0,7},{9,8},{10,9},{11,1... | collective-permute-start | bytes 2304008 | tf_op jit(solution)/shard_map/ppermute | solution.py:27
  47.8 7.0 %collective-permute-start.4 = (s32[64]{0:T(128)S(1)}, s32[64]{0:T(128)S(1)}, u32[]{:S(2)}, u32[]{:S(2)}) collective-permute-start(s32[64]{0:T(128)S(1)} %collective-permute-done.3), channel_id=1, source_target_pairs={{1,0},{2,1},{3,2},{4,3},{5,4},{6,5},{7,6},{0,7},{9,8},{10,9},{11,1... | collective-permute-start | bytes 776 | tf_op jit(solution)/shard_map/ppermute | solution.py:27
  54.8 6.5 %collective-permute-start.5 = (s32[64]{0:T(128)S(1)}, s32[64]{0:T(128)S(1)}, u32[]{:S(2)}, u32[]{:S(2)}) collective-permute-start(s32[64]{0:T(128)S(1)} %collective-permute-done.4), channel_id=1, source_target_pairs={{1,0},{2,1},{3,2},{4,3},{5,4},{6,5},{7,6},{0,7},{9,8},{10,9},{11,1... | collective-permute-start | bytes 776 | tf_op jit(solution)/shard_map/ppermute | solution.py:27
  61.4 9.5 %collective-permute-start.2 = (bf16[3000,128]{1,0:T(8,128)(2,1)S(1)}, bf16[3000,128]{1,0:T(8,128)(2,1)S(1)}, u32[]{:S(2)}, u32[]{:S(2)}) collective-permute-start(bf16[3000,128]{1,0:T(8,128)(2,1)S(1)} %collective-permute-done.1), channel_id=1, source_target_pairs={{1,0},{2,1},{3,2},{4,3},{5,4},{6,5},{7,6},{0,7},{9,8},{10,9},{11,1... | collective-permute-start | bytes 2304008 | tf_op jit(solution)/shard_map/ppermute | solution.py:27
  73.2 41.0 %copy-start = (s32[64]{0:T(128)S(1)}, s32[64]{0:T(128)}, u32[]{:S(2)}) copy-start(s32[64]{0:T(128)} %param.7) | copy-start | bytes 772
  114.8 5.5 %collective-permute-start.6 = (f32[64,128]{0,1:T(8,128)S(1)}, f32[64,128]{0,1:T(8,128)S(1)}, u32[]{:S(2)}, u32[]{:S(2)}) collective-permute-start(f32[64,128]{0,1:T(8,128)S(1)} %copy.14), channel_id=1, source_target_pairs={{0,16},{8,24},{16,0},{24,8},{1,17},{9,25},{17,1},{25,9},{2,18},{10... | collective-permute-start | bytes 98312 | tf_op jit(solution)/shard_map/ppermute | solution.py:21
  120.3 4.2 %collective-permute-start.7 = (f32[64,64]{0,1:T(8,128)S(1)}, f32[64,64]{0,1:T(8,128)S(1)}, u32[]{:S(2)}, u32[]{:S(2)}) collective-permute-start(f32[64,64]{0,1:T(8,128)S(1)} %get-tuple-element.201), channel_id=1, source_target_pairs={{7,0},{0,1},{1,2},{2,3},{3,4},{4,5},{5,6},{6,7},{15,8},{8,9},{9,10... | collective-permute-start | bytes 49160 | tf_op jit(solution)/shard_map/ppermute | solution.py:27
  120.3 4.9 %collective-permute-start.8 = (f32[64,64]{0,1:T(8,128)S(1)}, f32[64,64]{0,1:T(8,128)S(1)}, u32[]{:S(2)}, u32[]{:S(2)}) collective-permute-start(f32[64,64]{0,1:T(8,128)S(1)} %get-tuple-element.202), channel_id=1, source_target_pairs={{6,0},{7,1},{0,2},{1,3},{2,4},{3,5},{4,6},{5,7},{14,8},{15,9},{8,1... | collective-permute-start | bytes 49160 | tf_op jit(solution)/shard_map/ppermute | solution.py:27
where the time goes:
time: 126 us
  waiting for transfers between devices  55.1 us (44%)
  other arithmetic  23.4 us (19%)
  matrix products  20.2 us (16%)
  local copies, waits for them, and re-layouts  15.5 us (12%)
  starting transfers between devices  10.9 us (9%)
    ppermute x3, waiting for transfers between devices, partner_2(): return lax.ppermute(value, axis, pairs)  39.4 us
    ppermute x6, waiting for transfers between devices, from_behind(): return lax.ppermute(block, axis, route)  15.8 us
    dynamic_slice x9, local copies, waits for them, and re-layouts, one_group(): lax.dynamic_slice_in_dim(sine_table, first_shift, group_size, 0)[:, :, None]  9.4 us
    dot_general x9, matrix products, one_group(): lax.dot_general(rotated_low, column_both, contract, preferred_element_typ...  7.28 us
    dot_general x9, matrix products, one_group(): lax.dot_general(rotated_high, column_both, contract, preferred_element_ty...  7.25 us
    concatenate x9, other arithmetic, one_group(): rotated = jnp.concatenate([rotated_real, rotated_imag], axis=1)  6.91 us
    ppermute x6, starting transfers between devices, from_behind(): return lax.ppermute(block, axis, route)  6.76 us
    add x9, other arithmetic, one_group(): rotated_real = real_part[None] * cosine_rows + imag_part[None] * sine_rows  5.89 us
  transfers between devices with their start and end apart: 9, of which 6 were waited for; matrix products, arithmetic and copies ran while one was open for 12% of the time, Pallas kernels for 0%

commit v1 on v0

v1 whole, which is shorter than its diff:
```python
import math

import jax
import jax.numpy as jnp
from jax import lax
from jax.experimental import pallas as pl
from jax.experimental.pallas import tpu as pltpu
from jax.sharding import PartitionSpec as P

BOX = 24
RADIUS = 1
ROUND = 2
EPSILON = 1e-06
PAYLOAD = 32
LANES = 128
CUTS = (1024, 1024, 1024)
AXES = ("pair", "blk")
F32 = jnp.float32
BF16 = jnp.bfloat16

SHIFTS = tuple(
    (a, b, c)
    for a in range(-RADIUS, RADIUS + 1)
    for b in range(-RADIUS, RADIUS + 1)
    for c in range(-RADIUS, RADIUS + 1)
    if (a, b, c) > (0, 0, 0)
)
COUNT = len(SHIFTS)
VMEM = pl.BlockSpec(memory_space=pltpu.VMEM)
SMEM = pl.BlockSpec(memory_space=pltpu.SMEM)


def near_group(group):
    return (group >> 1 ^ group) & 1 == 0


def permute(value, route):
    pairs_n, blocks_n = lax.axis_size("pair"), lax.axis_size("blk")
    table = []
    for group in range(pairs_n):
        for block in range(blocks_n):
            place = route(group, block, blocks_n)
            if place is not None:
                source = place[0] * blocks_n + place[1] % blocks_n
                table.append((source, group * blocks_n + block))
    return lax.ppermute(value, AXES, table)


def cross_source(group, block, count):
    if near_group(group):
        return None
    return group ^ 1 ^ ROUND, block - 2 if block % 2 == 0 else block


def swap_source(group, block, count):
    if near_group(group):
        return group ^ 1, block + 4 if block % 2 == 0 else block - 2
    return group ^ 1, block if block % 2 == 0 else block - 2


def core_source(group, block, count):
    return group, block ^ 1


def own_back_source(group, block, count):
    if near_group(group):
        return None
    return group ^ 1 ^ ROUND, block + 2 if block % 2 == 0 else block


def first_back_source(group, block, count):
    if near_group(group):
        return group ^ 1, block if block % 2 == 0 else block + 2
    return group ^ ROUND, block - 2 if block % 2 == 0 else block + 2


def second_back_source(group, block, count):
    if near_group(group):
        return group ^ 1, block + 1
    return group ^ ROUND, block - 1 if block % 2 == 0 else block + 1


def wedge_rows(freqs, limits_ref):
    classes = limits_ref.shape[1]
    row = lax.broadcasted_iota(jnp.int32, (classes, 1), 0)
    same_side = jnp.zeros((classes, 1), jnp.int32)
    other_side = jnp.zeros((classes, 1), jnp.int32)
    for index in range(classes):
        same_side = jnp.where(row == index, limits_ref[0, index], same_side)
        other_side = jnp.where(row == index, limits_ref[1, index], other_side)
    first_axis, third_axis = freqs[0:1], freqs[2:3]
    limit = jnp.where(first_axis * third_axis >= 0, same_side, other_side)
    measured = 4 * third_axis * third_axis <= limit * (first_axis * first_axis)
    return jnp.where(measured, 1.0, 0.0).astype(F32)


def chosen_classes(ids_ref, classes):
    ids = ids_ref[...]
    both = jnp.concatenate([ids, ids], axis=1)
    row = lax.broadcasted_iota(jnp.int32, (classes, both.shape[1]), 0)
    return jnp.where(row == both, 1.0, 0.0).astype(F32), both


def mask_rows(spectra, table, chosen):
    measured = jnp.dot(
        table.T.astype(BF16), chosen.astype(BF16), preferred_element_type=F32
    )
    return spectra * measured


def first_mask_kernel(spectra_ref, ids_ref, limits_ref, freqs_ref, out_ref):
    rows = out_ref.shape[0]
    table = wedge_rows(freqs_ref[:, :rows], limits_ref)
    chosen, _ = chosen_classes(ids_ref, limits_ref.shape[1])
    out_ref[...] = mask_rows(spectra_ref[...].astype(F32), table, chosen).astype(BF16)


def split_three(value):
    high = value.astype(BF16).astype(F32)
    rest = value - high
    middle = rest.astype(BF16).astype(F32)
    return high, middle, rest - middle


def rest_mask_kernel(terms, starts, spectra_ref, ids_ref, limits_ref, freqs_ref, *out_refs):
    classes = limits_ref.shape[1]
    half = spectra_ref.shape[1] // 2
    table = wedge_rows(freqs_ref[...], limits_ref)
    chosen, both = chosen_classes(ids_ref, classes)
    spectra = spectra_ref[...].astype(F32)
    power = jnp.zeros((classes, half), F32)
    for index, start in enumerate(starts):
        rows = CUTS[index]
        used = min(rows, terms - start)
        part = spectra[start : start + used]
        if used < rows:
            part = jnp.concatenate([part, jnp.zeros((rows - used, 2 * half), F32)], axis=0)
        masked = mask_rows(part, table[:, start : start + rows], chosen)
        squared = masked * masked
        total = squared + pltpu.roll(squared, half, 1)
        table_part = table[:, start : start + rows].astype(BF16)
        for piece in split_three(total):
            power = power + jnp.dot(
                table_part, piece.astype(BF16), preferred_element_type=F32
            )[:, :half]
        if index == len(starts) - 1:
            pieces = [
                jnp.concatenate([piece, piece], axis=1) for piece in split_three(power)
            ]
            ids = jnp.broadcast_to(both.astype(F32), (classes, 2 * half))
            spare = jnp.zeros((rows - used - PAYLOAD, 2 * half), F32)
            masked = jnp.concatenate([masked[:used], *pieces, ids, spare], axis=0)
        if index > 0:
            out_refs[index - 1][...] = masked.astype(BF16)


def chunk_kernel(used, first, last, near_ref, kept_ref, crossed_ref, got_ref, core_ref,
                 trig_ref, *refs):
    if first:
        total_ref = None
    else:
        total_ref, *refs = refs
    outs, (high_ref, low_ref, other_ref) = refs[:-3], refs[-3:]
    rows, lanes = kept_ref.shape
    half = lanes // 2
    near = near_ref[0] == 1
    own = jnp.where(near, kept_ref[...].astype(F32), crossed_ref[...].astype(F32))
    got = got_ref[...].astype(F32)
    core = core_ref[...].astype(F32)
    other_ref[0:rows, :] = jnp.concatenate([got[:, :half], core[:, :half]], axis=1).astype(BF16)
    other_ref[rows:, :] = jnp.concatenate([got[:, half:], core[:, half:]], axis=1).astype(BF16)
    turned = own.T
    if used < rows:
        lane = lax.broadcasted_iota(jnp.int32, (1, rows), 1)
        turned = jnp.where(lane < used, turned, 0.0)
    real, imag = turned[:half], turned[half:]

    def put(row, part, value):
        high = value.astype(BF16)
        high_ref[row : row + half, part * rows : (part + 1) * rows] = high
        low_ref[row : row + half, part * rows : (part + 1) * rows] = (
            value - high.astype(F32)
        ).astype(BF16)

    plain = 2 * COUNT * half
    high_ref[plain:, 0:rows] = real.astype(BF16)
    high_ref[plain:, rows:] = imag.astype(BF16)
    for index in range(COUNT):
        cosine = trig_ref[index : index + 1, :]
        sine = trig_ref[COUNT + index : COUNT + index + 1, :]
        put(index * half, 0, cosine * real)
        put(index * half, 1, cosine * imag)
        put((COUNT + index) * half, 0, sine * imag)
        put((COUNT + index) * half, 1, -sine * real)
    scores_ref = outs[0]
    scores = jnp.dot(high_ref[...], other_ref[...], preferred_element_type=F32)
    if first:
        scores_ref[...] = scores
    else:
        scores_ref[...] = total_ref[...] + scores
    scores_ref[0:plain] += jnp.dot(low_ref[...], other_ref[...], preferred_element_type=F32)
    if not last:
        return

    largest = scores_ref[plain:]
    for index in range(COUNT):
        even = scores_ref[index * half : (index + 1) * half]
        odd = scores_ref[(COUNT + index) * half : (COUNT + index + 1) * half]
        largest = jnp.maximum(largest, even + jnp.abs(odd))
    classes = PAYLOAD // 4
    extra = slice(used, used + PAYLOAD)
    own_extra = own[extra][:, :half]
    other_extra = jnp.concatenate([got[extra][:, :half], core[extra][:, :half]], axis=1)

    def chosen(ids):
        row = lax.broadcasted_iota(jnp.int32, ids.shape, 0).astype(F32)
        once = jnp.where(row == ids, 1.0, 0.0).astype(F32)
        return jnp.concatenate([once] * 3, axis=0)

    own_chosen = chosen(own_extra[3 * classes :])
    other_chosen = chosen(other_extra[3 * classes :])
    row_norm = jnp.dot(
        own_extra[: 3 * classes].T.astype(BF16),
        other_chosen.astype(BF16),
        preferred_element_type=F32,
    )
    column_norm = jnp.dot(
        own_chosen.T.astype(BF16),
        other_extra[: 3 * classes].astype(BF16),
        preferred_element_type=F32,
    )
    best = largest * lax.rsqrt(row_norm * column_norm + EPSILON)
    outs[1][...] = best
    across = best.T
    outs[2][...] = across[:half]
    outs[3][...] = across[half:]


def chunk_scores(used, first, last, half, near, kept, crossed, got, core, trig, total):
    rows = kept.shape[0]
    score_rows = (2 * COUNT + 1) * half
    out_shape = [jax.ShapeDtypeStruct((score_rows, 2 * half), F32)]
    if last:
        out_shape += [
            jax.ShapeDtypeStruct((half, 2 * half), F32),
            jax.ShapeDtypeStruct((half, half), F32),
            jax.ShapeDtypeStruct((half, half), F32),
        ]
    operands = [near, kept, crossed, got, core, trig] + ([] if first else [total])
    return pl.pallas_call(
        lambda *refs: chunk_kernel(used, first, last, *refs),
        out_shape=out_shape,
        in_specs=[SMEM] + [VMEM] * (len(operands) - 1),
        out_specs=[VMEM] * len(out_shape),
        scratch_shapes=[
            pltpu.VMEM((score_rows, 2 * rows), BF16),
            pltpu.VMEM((score_rows - half, 2 * rows), BF16),
            pltpu.VMEM((2 * rows, 2 * half), BF16),
        ],
        compiler_params=pltpu.CompilerParams(vmem_limit_bytes=28 << 20),
        cost_estimate=pl.CostEstimate(
            flops=4 * score_rows * 2 * rows * 2 * half, bytes_accessed=4 << 20, transcendentals=0
        ),
    )(*operands)


def shards(spectra, wedge_ids, tilt_limits, term_freqs):
    terms, lanes = spectra.shape
    half = lanes // 2
    padded = sum(CUTS)
    starts = [sum(CUTS[:index]) for index in range(len(CUTS))]
    group, block = lax.axis_index("pair"), lax.axis_index("blk")
    near = near_group(group)
    near_flag = near.astype(jnp.int32)[None]
    ids = wedge_ids[None]
    limits = tilt_limits.T

    first_chunk = pl.pallas_call(
        first_mask_kernel,
        grid=(1,),
        out_shape=jax.ShapeDtypeStruct((CUTS[0], lanes), BF16),
        in_specs=[pl.BlockSpec((CUTS[0], lanes), lambda i: (0, 0)), VMEM, SMEM, VMEM],
        out_specs=VMEM,
    )(spectra, ids, limits, term_freqs)
    freqs = jnp.pad(term_freqs, ((0, 0), (0, padded - terms)))
    rest = pl.pallas_call(
        lambda *refs: rest_mask_kernel(terms, starts, *refs),
        out_shape=[jax.ShapeDtypeStruct((rows, lanes), BF16) for rows in CUTS[1:]],
        in_specs=[VMEM, VMEM, SMEM, VMEM],
        out_specs=[VMEM] * (len(CUTS) - 1),
    )(spectra, ids, limits, freqs)
    kept = [first_chunk, *rest]

    shift = jnp.array(SHIFTS, jnp.int32)
    turns = (
        shift[:, 0:1] * freqs[0:1] + shift[:, 1:2] * freqs[1:2] + shift[:, 2:3] * freqs[2:3]
    )
    angle = turns.astype(F32) * (2.0 * math.pi / BOX)
    trig = jnp.concatenate([jnp.cos(angle), jnp.sin(angle)], axis=0)

    crossed = [permute(chunk, cross_source) for chunk in kept]
    got, core = [], []
    for own, far in zip(kept, crossed):
        got.append(permute(jnp.where(near, own, far), swap_source))
        core.append(permute(got[-1], core_source))

    total = None
    for index, start in enumerate(starts):
        used = min(CUTS[index], terms - start)
        total, *tiles = chunk_scores(
            used, index == 0, index == len(starts) - 1, half, near_flag, kept[index],
            crossed[index], got[index], core[index], trig[:, start : start + CUTS[index]], total,
        )
    local, first_tile, second_tile = tiles
    returned = permute(local, own_back_source)
    first_back = permute(first_tile, first_back_source)
    second_back = permute(second_tile, second_back_source)

    mine = jnp.where(near, local, returned)
    got_tile, core_tile = mine[:, :half], mine[:, half:]
    even = block % 2 == 0
    lead = near == even
    return jnp.concatenate(
        [
            jnp.where(lead, second_back, core_tile),
            jnp.where(even, got_tile, first_back),
            jnp.where(lead, core_tile, second_back),
            jnp.where(even, first_back, got_tile),
        ],
        axis=1,
    )


def solution(mesh):
    placed = (P(None, AXES), P(AXES), P(), P())
    return jax.shard_map(
        shards, mesh=mesh, in_specs=placed, out_specs=P(AXES, None), check_vma=False
    )
```

time: 126 us -> 62 us (0.49)
  waiting for transfers between devices: 55.1 us -> 6.67 us
  other arithmetic: 23.4 us -> 1.74 us
  starting transfers between devices: 10.9 us -> 32.3 us
  matrix products: 20.2 us -> 0 us
  Pallas kernels: 0 us -> 18.6 us
  local copies, waits for them, and re-layouts: 15.5 us -> 1.93 us
    ppermute x9 -> x12, waiting for transfers between devices: 55.1 us -> 6.67 us  [permute(): return lax.ppermute(value, AXES, table)]
    ppermute x9 -> x12, starting transfers between devices: 10.9 us -> 32.3 us  [permute(): return lax.ppermute(value, AXES, table)]
    dot_general x24 -> x0, matrix products: 20.2 us -> none  [the longest x9 7.28 us: one_group(): lax.dot_general(rotated_low, column_both, contract, preferred_element_typ...]
    pallas_call x0 -> x5, Pallas kernels: none -> 18.6 us  [the longest x3 13.2 us: chunk_scores(): pl.pallas_call(lambda *refs: chunk_kernel(used, first, last, *refs), out_...]
    dynamic_slice x9 -> x0, local copies, waits for them, and re-layouts: 9.4 us -> none  [one_group(): lax.dynamic_slice_in_dim(sine_table, first_shift, group_size, 0)[:, :, None]]
    concatenate x13 -> x2, other arithmetic: 9.34 us -> 0.76 us  [the longest x1 0.73 us: shards(): jnp.concatenate([jnp.where(lead, second_back, core_tile), jnp.where(even,...]
    add x9 -> x0, other arithmetic: 5.89 us -> none  [one_group(): rotated_real = real_part[None] * cosine_rows + imag_part[None] * sine_rows]
    convert_element_type x10 -> x0, other arithmetic: 5.35 us -> none  [the longest x9 3.41 us: one_group(): (rotated - rotated_high.astype(jnp.float32)).astype(jnp.bfloat16)]
  transfers between devices with their start and end apart: 9 -> 12, of which waited for: 6 -> 4; matrix products, arithmetic and copies ran while one was open for 12% -> 4% of each run, Pallas kernels for 0% -> 19%
where the time goes in v1:
time: 62 us; the launch traced here: 61.4 us
  starting transfers between devices  32.3 us (52%)
  Pallas kernels  18.6 us (30%)
  waiting for transfers between devices  6.67 us (11%)
  local copies, waits for them, and re-layouts  1.93 us (3%)
  other arithmetic  1.74 us (3%)
    ppermute x12, starting transfers between devices, permute(): return lax.ppermute(value, AXES, table)  32.3 us
    pallas_call x3, Pallas kernels, chunk_scores(): pl.pallas_call(lambda *refs: chunk_kernel(used, first, last, *refs), out_...  13.2 us
    ppermute x12, waiting for transfers between devices, permute(): return lax.ppermute(value, AXES, table)  6.67 us
    pallas_call x1, Pallas kernels, shards(): pl.pallas_call(lambda *refs: rest_mask_kernel(terms, starts, *refs), out_...  3.4 us
    pallas_call x1, Pallas kernels, shards(): pl.pallas_call(first_mask_kernel, grid=(1,), out_shape=jax.ShapeDtypeStru...  1.99 us
  transfers between devices with their start and end apart: 12, of which 4 were waited for; matrix products, arithmetic and copies ran while one was open for 4% of the time, Pallas kernels for 19%

profile of v1, /device:TPU:0, one launch (start us, length us, event | category | flops | bytes accessed | tf_op | source)
XLA Modules:
  0.0 61.4 jit_solution(14578805843489696314)
XLA Ops:
  0.0 0.0 copy-start.3
  0.0 2.0 %shard_map.56.refs_1_ = bf16[1024,128]{1,0:T(8,128)(2,1)} custom-call(bf16[3000,128]{1,0:T(8,128)(2,1)} %spectra_ref.1, s32[1,64]{1,0:T(1,128)} %bitcast.11, s32[2,8]{1,0:T(2,128)} %bitcast.9, s32[3,3000]{1,0:T(4,128)} %freqs_ref.1), custom_call_target="tpu_custom_call" | custom-call | tf_op jit(solution)/shard_map/pallas_call | solution.py:278
  2.0 0.7 %collective-permute-start.6 = (bf16[1024,128]{1,0:T(8,128)(2,1)}, bf16[1024,128]{1,0:T(8,128)(2,1)S(1)}, u32[]{:S(2)}, u32[]{:S(2)}) collective-permute-start(bf16[1024,128]{1,0:T(8,128)(2,1)} %shard_map.56.refs_1_), channel_id=1, source_target_pairs={{22,8},{17,9},{16,10},{19,11},{18,12},{21,13},{20,14},{23,15},{14,... | collective-permute-start | bytes 786440 | tf_op jit(solution)/shard_map/ppermute | solution.py:46
  2.7 0.0 copy-done.3
  2.7 0.6 %pad.4.refs_3_ = s32[3,3072]{1,0:T(4,128)} pad(s32[3,3000]{1,0:T(4,128)S(1)} %copy-done.3, s32[]{:T(128)} %constant.23.clone.1), padding=0_0x0_72 | pad | bytes 72868 | tf_op jit(solution)/shard_map/jit(_pad)/pad | solution.py:285
  3.3 0.0 copy-start
  3.3 3.4 %shard_map.55 = (bf16[1024,128]{1,0:T(8,128)(2,1)}, bf16[1024,128]{1,0:T(8,128)(2,1)}) custom-call(bf16[3000,128]{1,0:T(8,128)(2,1)} %spectra_ref.1, s32[1,64]{1,0:T(1,128)} %bitcast.12, s32[2,8]{1,0:T(2,128)} %bitcast.10, s32[3,3072]{1,0:T(4,128)} %pad.4.refs_3_), custom_call_target="tpu_custom_call" | custom-call | tf_op jit(solution)/shard_map/pallas_call | solution.py:286
  6.7 0.7 %collective-permute-start.3 = (bf16[1024,128]{1,0:T(8,128)(2,1)}, bf16[1024,128]{1,0:T(8,128)(2,1)S(1)}, u32[]{:S(2)}, u32[]{:S(2)}) collective-permute-start(bf16[1024,128]{1,0:T(8,128)(2,1)} %get-tuple-element.11.refs_1_), channel_id=1, source_target_pairs={{22,8},{17,9},{16,10},{19,11},{18,12},{21,13},{20,14},{23,15},{14,... | collective-permute-start | bytes 786440 | tf_op jit(solution)/shard_map/ppermute | solution.py:46
  7.4 0.7 %collective-permute-start = (bf16[1024,128]{1,0:T(8,128)(2,1)}, bf16[1024,128]{1,0:T(8,128)(2,1)S(1)}, u32[]{:S(2)}, u32[]{:S(2)}) collective-permute-start(bf16[1024,128]{1,0:T(8,128)(2,1)} %get-tuple-element.10.refs_1_), channel_id=1, source_target_pairs={{22,8},{17,9},{16,10},{19,11},{18,12},{21,13},{20,14},{23,15},{14,... | collective-permute-start | bytes 786440 | tf_op jit(solution)/shard_map/ppermute | solution.py:46
  8.1 0.6 %pad_slice_fusion.6 = (s32[1,3072]{1,0:T(1,128)S(1)}, s32[1,3072]{1,0:T(1,128)}, s32[1,3072]{1,0:T(1,128)}) fusion(s32[3,3000]{1,0:T(4,128)S(1)} %copy-done.3), kind=kLoop, calls=%fused_computation.21 | loop fusion | bytes 72864 | tf_op jit(solution)/shard_map/slice | solution.py:296
  8.7 0.0 copy-start.2
  8.7 0.0 collective-permute-done.6.refs_2_
  8.7 0.0 copy-done
  8.7 0.0 copy-start.1
  8.8 13.2 %collective-permute-start.7 = (bf16[1024,128]{1,0:T(8,128)(2,1)S(1)}, bf16[1024,128]{1,0:T(8,128)(2,1)S(1)}, u32[]{:S(2)}, u32[]{:S(2)}) collective-permute-start(bf16[1024,128]{1,0:T(8,128)(2,1)S(1)} %broadcast_select_fusion), channel_id=1, source_target_pairs={{12,0},{15,1},{14,2},{9,3},{8,4},{11,5},{10,6},{13,7},{0,8},{7,9},... | collective-permute-start | bytes 786440 | tf_op jit(solution)/shard_map/ppermute | solution.py:46
  21.9 0.0 collective-permute-done.3.refs_2_
  21.9 0.0 copy-done.2
  21.9 5.6 %collective-permute-start.4 = (bf16[1024,128]{1,0:T(8,128)(2,1)S(1)}, bf16[1024,128]{1,0:T(8,128)(2,1)S(1)}, u32[]{:S(2)}, u32[]{:S(2)}) collective-permute-start(bf16[1024,128]{1,0:T(8,128)(2,1)S(1)} %broadcast_select_fusion.1), channel_id=1, source_target_pairs={{12,0},{15,1},{14,2},{9,3},{8,4},{11,5},{10,6},{13,7},{0,8},{7,9},... | collective-permute-start | bytes 786440 | tf_op jit(solution)/shard_map/ppermute | solution.py:46
  27.6 0.0 collective-permute-done.refs_2_
  27.6 0.0 copy-done.1
  27.6 0.0 copy-start.4
  27.6 0.0 copy-start.5
  27.6 5.4 %collective-permute-start.1 = (bf16[1024,128]{1,0:T(8,128)(2,1)S(1)}, bf16[1024,128]{1,0:T(8,128)(2,1)S(1)}, u32[]{:S(2)}, u32[]{:S(2)}) collective-permute-start(bf16[1024,128]{1,0:T(8,128)(2,1)S(1)} %broadcast_select_fusion.2), channel_id=1, source_target_pairs={{12,0},{15,1},{14,2},{9,3},{8,4},{11,5},{10,6},{13,7},{0,8},{7,9},... | collective-permute-start | bytes 786440 | tf_op jit(solution)/shard_map/ppermute | solution.py:46
  33.1 0.0 collective-permute-done.7.refs_3_
  33.1 0.0 collective-permute-start.8
  33.1 0.0 copy-start.6
  33.1 0.0 copy-start.7
  33.1 0.0 copy-start.8
  33.1 0.0 copy-done.4
  33.1 0.0 copy-done.5
  33.1 0.6 copy-done.6
  33.7 0.0 copy-done.7
  33.7 0.0 copy-done.8
  33.8 0.8 %fusion = (f32[13,3072]{1,0:T(8,128)S(1)}, f32[13,3072]{1,0:T(8,128)S(1)}) fusion(s32[3072]{0:T(1024)S(1)} %bitcast.8, s32[13]{0:T(128)S(1)} %copy-done.8, s32[3072]{0:T(1024)S(1)} %bitcast.7, s32[13]{0:T(128)S(1)} %copy-done.7, s32[3072]{0:T(1024)S(1)} %bitcast.6, s32[13]{0:T(128)S(1)} %copy-done.6), kind=kLoop, calls=%fused_computation.8 | loop fusion | flops 279552 | bytes 356508 | tf_op jit(solution)/shard_map/sin | solution.py:299
  34.6 0.3 collective-permute-done.4.refs_3_
  34.9 0.3 collective-permute-start.5
  35.2 3.0 %collective-permute-done.1.refs_3_ = bf16[1024,128]{1,0:T(8,128)(2,1)S(1)} collective-permute-done((bf16[1024,128]{1,0:T(8,128)(2,1)S(1)}, bf16[1024,128]{1,0:T(8,128)(2,1)S(1)}, u32[]{:S(2)}, u32[]{:S(2)}) %collective-permute-start.1) | collective-permute-done | bytes 262176 | tf_op jit(solution)/shard_map/ppermute | solution.py:46
  38.2 0.0 collective-permute-start.2
  38.2 0.0 collective-permute-done.8.refs_4_
  38.2 4.0 %shard_map.57.refs_6_ = f32[1728,128]{1,0:T(8,128)S(1)} custom-call(s32[1]{0:T(128)} %bitcast.refs_0_, bf16[1024,128]{1,0:T(8,128)(2,1)S(1)} %copy-done, bf16[1024,128]{1,0:T(8,128)(2,1)S(1)} %collective-permute-done.6.refs_2_, bf16[1024,128]{1,0:T(8,128)(2,1)S(1)} %collective-permute-done.7.refs_3_, bf16[1024,128]{1,0:T(8,128)(2,1)S(1)} %collective-permute-done.8.refs_4_, ...), custom_call_target="tpu_custom_call" | custom-call | flops 1811939328 | bytes 4194304 | tf_op jit(solution)/shard_map/pallas_call | solution.py:250
  42.3 0.0 collective-permute-done.5.refs_4_
  42.3 4.1 %shard_map.58.refs_6_ = f32[1728,128]{1,0:T(8,128)S(1)} custom-call(s32[1]{0:T(128)} %bitcast.refs_0_, bf16[1024,128]{1,0:T(8,128)(2,1)S(1)} %copy-done.2, bf16[1024,128]{1,0:T(8,128)(2,1)S(1)} %collective-permute-done.3.refs_2_, bf16[1024,128]{1,0:T(8,128)(2,1)S(1)} %collective-permute-done.4.refs_3_, bf16[1024,128]{1,0:T(8,128)(2,1)S(1)} %collective-permute-done.5.refs_4_, ...), custom_call_target="tpu_custom_call" | custom-call | flops 1811939328 | bytes 4194304 | tf_op jit(solution)/shard_map/pallas_call | solution.py:250
  46.3 0.0 collective-permute-done.2.refs_4_
  46.3 5.1 %shard_map.59 = (f32[1728,128]{1,0:T(8,128)}, f32[64,128]{1,0:T(8,128)S(1)}, f32[64,64]{1,0:T(8,128)S(1)}, f32[64,64]{1,0:T(8,128)S(1)}) custom-call(s32[1]{0:T(128)} %bitcast.refs_0_, bf16[1024,128]{1,0:T(8,128)(2,1)S(1)} %copy-done.1, bf16[1024,128]{1,0:T(8,128)(2,1)S(1)} %collective-permute-done.refs_2_, ...), custom_call_target="tpu_custom_call" | custom-call | flops 1811939328 | bytes 4194304 | tf_op jit(solution)/shard_map/pallas_call | solution.py:250
  51.5 0.7 %collective-permute-start.10 = (f32[64,128]{1,0:T(8,128)S(1)}, f32[64,128]{1,0:T(8,128)S(1)}, u32[]{:S(2)}, u32[]{:S(2)}) collective-permute-start(f32[64,128]{1,0:T(8,128)S(1)} %get-tuple-element.13), channel_id=1, source_target_pairs={{18,8},{17,9},{20,10},{19,11},{22,12},{21,13},{16,14},{23,15},{10,... | collective-permute-start | bytes 98312 | tf_op jit(solution)/shard_map/ppermute | solution.py:46
  52.1 5.1 %collective-permute-start.11 = (f32[64,64]{1,0:T(8,128)S(1)}, f32[64,64]{1,0:T(8,128)S(1)}, u32[]{:S(2)}, u32[]{:S(2)}) collective-permute-start(f32[64,64]{1,0:T(8,128)S(1)} %get-tuple-element.14), channel_id=1, source_target_pairs={{8,0},{11,1},{10,2},{13,3},{12,4},{15,5},{14,6},{9,7},{30,8},{27,9... | collective-permute-start | bytes 49160 | tf_op jit(solution)/shard_map/ppermute | solution.py:46
  57.2 0.0 collective-permute-start.9
  57.3 0.0 collective-permute-done.10
  57.3 1.6 %collective-permute-done.11 = f32[64,64]{1,0:T(8,128)S(1)} collective-permute-done((f32[64,64]{1,0:T(8,128)S(1)}, f32[64,64]{1,0:T(8,128)S(1)}, u32[]{:S(2)}, u32[]{:S(2)}) %collective-permute-start.11) | collective-permute-done | bytes 16416 | tf_op jit(solution)/shard_map/ppermute | solution.py:46
  58.8 1.7 %collective-permute-done.9 = f32[64,64]{1,0:T(8,128)S(1)} collective-permute-done((f32[64,64]{1,0:T(8,128)S(1)}, f32[64,64]{1,0:T(8,128)S(1)}, u32[]{:S(2)}, u32[]{:S(2)}) %collective-permute-start.9) | collective-permute-done | bytes 16416 | tf_op jit(solution)/shard_map/ppermute | solution.py:46
  60.6 0.1 slice_select_fusion.3
  60.7 0.7 %pad_maximum_fusion.1 = f32[64,256]{1,0:T(8,128)} fusion(f32[64,64]{1,0:T(8,128)S(1)} %get-tuple-element.27, f32[64,64]{1,0:T(8,128)S(1)} %get-tuple-element.19, f32[64,64]{1,0:T(8,128)S(1)} %get-tuple-element.28, f32[64,64]{1,0:T(8,128)S(1)} %get-tuple-element.18), kind=kLoop, calls=%fused_computation.13 | loop fusion | flops 49152 | bytes 131072 | tf_op jit(solution)/shard_map/concatenate | solution.py:323
  (5 shorter events, 0.1 us)
Async XLA Ops:
  0.0 2.7 %copy-start.3 = (s32[3,3000]{1,0:T(4,128)S(1)}, s32[3,3000]{1,0:T(4,128)}, u32[]{:S(2)}) copy-start(s32[3,3000]{1,0:T(4,128)} %freqs_ref.1) | copy-start | bytes 108004
  2.0 6.7 %collective-permute-start.6 = (bf16[1024,128]{1,0:T(8,128)(2,1)}, bf16[1024,128]{1,0:T(8,128)(2,1)S(1)}, u32[]{:S(2)}, u32[]{:S(2)}) collective-permute-start(bf16[1024,128]{1,0:T(8,128)(2,1)} %shard_map.56.refs_1_), channel_id=1, source_target_pairs={{22,8},{17,9},{16,10},{19,11},{18,12},{21,13},{20,14},{23,15},{14,... | collective-permute-start | bytes 786440 | tf_op jit(solution)/shard_map/ppermute | solution.py:46
  3.3 5.4 %copy-start = (bf16[1024,128]{1,0:T(8,128)(2,1)S(1)}, bf16[1024,128]{1,0:T(8,128)(2,1)}, u32[]{:S(2)}) copy-start(bf16[1024,128]{1,0:T(8,128)(2,1)} %shard_map.56.refs_1_) | copy-start | bytes 786436
  6.7 15.2 %collective-permute-start.3 = (bf16[1024,128]{1,0:T(8,128)(2,1)}, bf16[1024,128]{1,0:T(8,128)(2,1)S(1)}, u32[]{:S(2)}, u32[]{:S(2)}) collective-permute-start(bf16[1024,128]{1,0:T(8,128)(2,1)} %get-tuple-element.11.refs_1_), channel_id=1, source_target_pairs={{22,8},{17,9},{16,10},{19,11},{18,12},{21,13},{20,14},{23,15},{14,... | collective-permute-start | bytes 786440 | tf_op jit(solution)/shard_map/ppermute | solution.py:46
  7.4 20.2 %collective-permute-start = (bf16[1024,128]{1,0:T(8,128)(2,1)}, bf16[1024,128]{1,0:T(8,128)(2,1)S(1)}, u32[]{:S(2)}, u32[]{:S(2)}) collective-permute-start(bf16[1024,128]{1,0:T(8,128)(2,1)} %get-tuple-element.10.refs_1_), channel_id=1, source_target_pairs={{22,8},{17,9},{16,10},{19,11},{18,12},{21,13},{20,14},{23,15},{14,... | collective-permute-start | bytes 786440 | tf_op jit(solution)/shard_map/ppermute | solution.py:46
  8.7 13.2 %copy-start.2 = (bf16[1024,128]{1,0:T(8,128)(2,1)S(1)}, bf16[1024,128]{1,0:T(8,128)(2,1)}, u32[]{:S(2)}) copy-start(bf16[1024,128]{1,0:T(8,128)(2,1)} %get-tuple-element.11.refs_1_) | copy-start | bytes 786436
  8.7 18.8 %copy-start.1 = (bf16[1024,128]{1,0:T(8,128)(2,1)S(1)}, bf16[1024,128]{1,0:T(8,128)(2,1)}, u32[]{:S(2)}) copy-start(bf16[1024,128]{1,0:T(8,128)(2,1)} %get-tuple-element.10.refs_1_) | copy-start | bytes 786436
  8.8 24.3 %collective-permute-start.7 = (bf16[1024,128]{1,0:T(8,128)(2,1)S(1)}, bf16[1024,128]{1,0:T(8,128)(2,1)S(1)}, u32[]{:S(2)}, u32[]{:S(2)}) collective-permute-start(bf16[1024,128]{1,0:T(8,128)(2,1)S(1)} %broadcast_select_fusion), channel_id=1, source_target_pairs={{12,0},{15,1},{14,2},{9,3},{8,4},{11,5},{10,6},{13,7},{0,8},{7,9},... | collective-permute-start | bytes 786440 | tf_op jit(solution)/shard_map/ppermute | solution.py:46
  21.9 12.9 %collective-permute-start.4 = (bf16[1024,128]{1,0:T(8,128)(2,1)S(1)}, bf16[1024,128]{1,0:T(8,128)(2,1)S(1)}, u32[]{:S(2)}, u32[]{:S(2)}) collective-permute-start(bf16[1024,128]{1,0:T(8,128)(2,1)S(1)} %broadcast_select_fusion.1), channel_id=1, source_target_pairs={{12,0},{15,1},{14,2},{9,3},{8,4},{11,5},{10,6},{13,7},{0,8},{7,9},... | collective-permute-start | bytes 786440 | tf_op jit(solution)/shard_map/ppermute | solution.py:46
  27.6 5.5 %copy-start.4 = (s32[1,3072]{1,0:T(1,128)S(1)}, s32[1,3072]{1,0:T(1,128)}, u32[]{:S(2)}) copy-start(s32[1,3072]{1,0:T(1,128)} %get-tuple-element.23) | copy-start | bytes 36868
  27.6 5.5 %copy-start.5 = (s32[1,3072]{1,0:T(1,128)S(1)}, s32[1,3072]{1,0:T(1,128)}, u32[]{:S(2)}) copy-start(s32[1,3072]{1,0:T(1,128)} %get-tuple-element.24) | copy-start | bytes 36868
  27.6 10.6 %collective-permute-start.1 = (bf16[1024,128]{1,0:T(8,128)(2,1)S(1)}, bf16[1024,128]{1,0:T(8,128)(2,1)S(1)}, u32[]{:S(2)}, u32[]{:S(2)}) collective-permute-start(bf16[1024,128]{1,0:T(8,128)(2,1)S(1)} %broadcast_select_fusion.2), channel_id=1, source_target_pairs={{12,0},{15,1},{14,2},{9,3},{8,4},{11,5},{10,6},{13,7},{0,8},{7,9},... | collective-permute-start | bytes 786440 | tf_op jit(solution)/shard_map/ppermute | solution.py:46
  33.1 5.2 %collective-permute-start.8 = (bf16[1024,128]{1,0:T(8,128)(2,1)S(1)}, bf16[1024,128]{1,0:T(8,128)(2,1)S(1)}, u32[]{:S(2)}, u32[]{:S(2)}) collective-permute-start(bf16[1024,128]{1,0:T(8,128)(2,1)S(1)} %collective-permute-done.7.refs_3_), channel_id=1, source_target_pairs={{1,0},{0,1},{3,2},{2,3},{5,4},{4,5},{7,6},{6,7},{9,8},{8,9},{11,10... | collective-permute-start | bytes 786440 | tf_op jit(solution)/shard_map/ppermute | solution.py:46
  33.1 0.7 %copy-start.6 = (s32[13]{0:T(128)S(1)}, s32[13]{0:T(128)}, u32[]{:S(2)}) copy-start(s32[13]{0:T(128)} %constant.31) | copy-start | bytes 160
  33.1 0.7 %copy-start.7 = (s32[13]{0:T(128)S(1)}, s32[13]{0:T(128)}, u32[]{:S(2)}) copy-start(s32[13]{0:T(128)} %constant.33) | copy-start | bytes 160
  33.1 0.7 %copy-start.8 = (s32[13]{0:T(128)S(1)}, s32[13]{0:T(128)}, u32[]{:S(2)}) copy-start(s32[13]{0:T(128)} %constant.35) | copy-start | bytes 160
  34.9 7.4 %collective-permute-start.5 = (bf16[1024,128]{1,0:T(8,128)(2,1)S(1)}, bf16[1024,128]{1,0:T(8,128)(2,1)S(1)}, u32[]{:S(2)}, u32[]{:S(2)}) collective-permute-start(bf16[1024,128]{1,0:T(8,128)(2,1)S(1)} %collective-permute-done.4.refs_3_), channel_id=1, source_target_pairs={{1,0},{0,1},{3,2},{2,3},{5,4},{4,5},{7,6},{6,7},{9,8},{8,9},{11,10... | collective-permute-start | bytes 786440 | tf_op jit(solution)/shard_map/ppermute | solution.py:46
  38.2 8.1 %collective-permute-start.2 = (bf16[1024,128]{1,0:T(8,128)(2,1)S(1)}, bf16[1024,128]{1,0:T(8,128)(2,1)S(1)}, u32[]{:S(2)}, u32[]{:S(2)}) collective-permute-start(bf16[1024,128]{1,0:T(8,128)(2,1)S(1)} %collective-permute-done.1.refs_3_), channel_id=1, source_target_pairs={{1,0},{0,1},{3,2},{2,3},{5,4},{4,5},{7,6},{6,7},{9,8},{8,9},{11,10... | collective-permute-start | bytes 786440 | tf_op jit(solution)/shard_map/ppermute | solution.py:46
  51.5 5.8 %collective-permute-start.10 = (f32[64,128]{1,0:T(8,128)S(1)}, f32[64,128]{1,0:T(8,128)S(1)}, u32[]{:S(2)}, u32[]{:S(2)}) collective-permute-start(f32[64,128]{1,0:T(8,128)S(1)} %get-tuple-element.13), channel_id=1, source_target_pairs={{18,8},{17,9},{20,10},{19,11},{22,12},{21,13},{16,14},{23,15},{10,... | collective-permute-start | bytes 98312 | tf_op jit(solution)/shard_map/ppermute | solution.py:46
  52.1 6.7 %collective-permute-start.11 = (f32[64,64]{1,0:T(8,128)S(1)}, f32[64,64]{1,0:T(8,128)S(1)}, u32[]{:S(2)}, u32[]{:S(2)}) collective-permute-start(f32[64,64]{1,0:T(8,128)S(1)} %get-tuple-element.14), channel_id=1, source_target_pairs={{8,0},{11,1},{10,2},{13,3},{12,4},{15,5},{14,6},{9,7},{30,8},{27,9... | collective-permute-start | bytes 49160 | tf_op jit(solution)/shard_map/ppermute | solution.py:46
  57.2 3.3 %collective-permute-start.9 = (f32[64,64]{1,0:T(8,128)S(1)}, f32[64,64]{1,0:T(8,128)S(1)}, u32[]{:S(2)}, u32[]{:S(2)}) collective-permute-start(f32[64,64]{1,0:T(8,128)S(1)} %get-tuple-element.12), channel_id=1, source_target_pairs={{9,0},{10,1},{11,2},{12,3},{13,4},{14,5},{15,6},{8,7},{31,8},{26,9... | collective-permute-start | bytes 49160 | tf_op jit(solution)/shard_map/ppermute | solution.py:46

commit v2 on v1

--- a/solution.py
+++ b/solution.py
@@ -1,3 +1,4 @@
+import functools
 import math
 
 import jax
@@ -26,8 +27,11 @@
     if (a, b, c) > (0, 0, 0)
 )
 COUNT = len(SHIFTS)
+SHIFT_ROWS = 16
 VMEM = pl.BlockSpec(memory_space=pltpu.VMEM)
 SMEM = pl.BlockSpec(memory_space=pltpu.SMEM)
+ANY = pl.BlockSpec(memory_space=pl.ANY)
+LOW_COST = pl.CostEstimate(flops=1, bytes_accessed=1, transcendentals=0)
 
 
 def near_group(group):
@@ -76,8 +80,16 @@
 
 def second_back_source(group, block, count):
     if near_group(group):
-        return group ^ 1, block + 1
-    return group ^ ROUND, block - 1 if block % 2 == 0 else block + 1
+        return group, block ^ 1
+    return group ^ 1 ^ ROUND, block + 3 if block % 2 == 0 else block - 1
+
+
+def chunk_freqs(freqs_ref, start, rows):
+    axes, terms = freqs_ref.shape
+    if start + rows <= terms:
+        return freqs_ref[:, start : start + rows]
+    spare = jnp.zeros((axes, start + rows - terms), jnp.int32)
+    return jnp.concatenate([freqs_ref[:, start:], spare], axis=1)
 
 
 def wedge_rows(freqs, limits_ref):
@@ -122,54 +134,66 @@
     return high, middle, rest - middle
 
 
-def rest_mask_kernel(terms, starts, spectra_ref, ids_ref, limits_ref, freqs_ref, *out_refs):
+def rest_mask_kernel(terms, starts, spectra_ref, ids_ref, limits_ref, freqs_ref, done_ref,
+                     *out_refs):
     classes = limits_ref.shape[1]
     half = spectra_ref.shape[1] // 2
-    table = wedge_rows(freqs_ref[...], limits_ref)
     chosen, both = chosen_classes(ids_ref, classes)
     spectra = spectra_ref[...].astype(F32)
     power = jnp.zeros((classes, half), F32)
-    for index, start in enumerate(starts):
-        rows = CUTS[index]
+    for index, (rows, start) in enumerate(zip(CUTS, starts)):
         used = min(rows, terms - start)
-        part = spectra[start : start + used]
-        if used < rows:
-            part = jnp.concatenate([part, jnp.zeros((rows - used, 2 * half), F32)], axis=0)
-        masked = mask_rows(part, table[:, start : start + rows], chosen)
+        table = wedge_rows(chunk_freqs(freqs_ref, start, rows), limits_ref)
+        if index == 0:
+            masked = done_ref[...].astype(F32)
+        else:
+            part = spectra[start : start + used]
+            if used < rows:
+                part = jnp.concatenate([part, jnp.zeros((rows - used, 2 * half), F32)], axis=0)
+            masked = mask_rows(part, table, chosen)
         squared = masked * masked
         total = squared + pltpu.roll(squared, half, 1)
-        table_part = table[:, start : start + rows].astype(BF16)
+        table_part = table.astype(BF16)
         for piece in split_three(total):
             power = power + jnp.dot(
                 table_part, piece.astype(BF16), preferred_element_type=F32
             )[:, :half]
-        if index == len(starts) - 1:
-            pieces = [
-                jnp.concatenate([piece, piece], axis=1) for piece in split_three(power)
-            ]
-            ids = jnp.broadcast_to(both.astype(F32), (classes, 2 * half))
-            spare = jnp.zeros((rows - used - PAYLOAD, 2 * half), F32)
-            masked = jnp.concatenate([masked[:used], *pieces, ids, spare], axis=0)
-        if index > 0:
+        if 0 < index < len(CUTS) - 1:
             out_refs[index - 1][...] = masked.astype(BF16)
-
-
-def chunk_kernel(used, first, last, near_ref, kept_ref, crossed_ref, got_ref, core_ref,
-                 trig_ref, *refs):
+    pieces = [jnp.concatenate([piece, piece], axis=1) for piece in split_three(power)]
+    ids = jnp.broadcast_to(both.astype(F32), (classes, 2 * half))
+    spare = jnp.zeros((rows - used - PAYLOAD, 2 * half), F32)
+    masked = jnp.concatenate([masked[:used], *pieces, ids, spare], axis=0)
+    out_refs[-1][...] = masked.astype(BF16)
+
+
+def phase_kernel(starts, freqs_ref, _, *out_refs):
+    for rows, start, out_ref in zip(CUTS, starts, out_refs):
+        freqs = chunk_freqs(freqs_ref, start, rows).astype(F32)
+        turns = jnp.concatenate(
+            [a * freqs[0:1] + b * freqs[1:2] + c * freqs[2:3] for a, b, c in SHIFTS]
+            + [jnp.zeros((SHIFT_ROWS - COUNT, rows), F32)],
+            axis=0,
+        )
+        angle = turns * (2.0 * math.pi / BOX)
+        out_ref[:SHIFT_ROWS] = jnp.cos(angle)
+        out_ref[SHIFT_ROWS:] = jnp.sin(angle)
+
+
+def chunk_kernel(used, first, last, got_ref, sent_ref, core_ref, trig_ref, *refs):
     if first:
         total_ref = None
     else:
         total_ref, *refs = refs
     outs, (high_ref, low_ref, other_ref) = refs[:-3], refs[-3:]
-    rows, lanes = kept_ref.shape
+    rows, lanes = got_ref.shape
     half = lanes // 2
-    near = near_ref[0] == 1
-    own = jnp.where(near, kept_ref[...].astype(F32), crossed_ref[...].astype(F32))
     got = got_ref[...].astype(F32)
+    sent = sent_ref[...].astype(F32)
     core = core_ref[...].astype(F32)
-    other_ref[0:rows, :] = jnp.concatenate([got[:, :half], core[:, :half]], axis=1).astype(BF16)
-    other_ref[rows:, :] = jnp.concatenate([got[:, half:], core[:, half:]], axis=1).astype(BF16)
-    turned = own.T
+    other_ref[0:rows, :] = jnp.concatenate([sent[:, :half], core[:, :half]], axis=1).astype(BF16)
+    other_ref[rows:, :] = jnp.concatenate([sent[:, half:], core[:, half:]], axis=1).astype(BF16)
+    turned = got.T
     if used < rows:
         lane = lax.broadcasted_iota(jnp.int32, (1, rows), 1)
         turned = jnp.where(lane < used, turned, 0.0)
@@ -187,7 +211,7 @@
     high_ref[plain:, rows:] = imag.astype(BF16)
     for index in range(COUNT):
         cosine = trig_ref[index : index + 1, :]
-        sine = trig_ref[COUNT + index : COUNT + index + 1, :]
+        sine = trig_ref[SHIFT_ROWS + index : SHIFT_ROWS + index + 1, :]
         put(index * half, 0, cosine * real)
         put(index * half, 1, cosine * imag)
         put((COUNT + index) * half, 0, sine * imag)
@@ -209,8 +233,8 @@
         largest = jnp.maximum(largest, even + jnp.abs(odd))
     classes = PAYLOAD // 4
     extra = slice(used, used + PAYLOAD)
-    own_extra = own[extra][:, :half]
-    other_extra = jnp.concatenate([got[extra][:, :half], core[extra][:, :half]], axis=1)
+    own_extra = got[extra][:, :half]
+    other_extra = jnp.concatenate([sent[extra][:, :half], core[extra][:, :half]], axis=1)
 
     def chosen(ids):
         row = lax.broadcasted_iota(jnp.int32, ids.shape, 0).astype(F32)
@@ -236,8 +260,8 @@
     outs[3][...] = across[half:]
 
 
-def chunk_scores(used, first, last, half, near, kept, crossed, got, core, trig, total):
-    rows = kept.shape[0]
+def chunk_scores(used, first, last, half, got, sent, core, trig, total):
+    rows = got.shape[0]
     score_rows = (2 * COUNT + 1) * half
     out_shape = [jax.ShapeDtypeStruct((score_rows, 2 * half), F32)]
     if last:
@@ -246,11 +270,11 @@
             jax.ShapeDtypeStruct((half, half), F32),
             jax.ShapeDtypeStruct((half, half), F32),
         ]
-    operands = [near, kept, crossed, got, core, trig] + ([] if first else [total])
+    operands = [got, sent, core, trig] + ([] if first else [total])
     return pl.pallas_call(
         lambda *refs: chunk_kernel(used, first, last, *refs),
         out_shape=out_shape,
-        in_specs=[SMEM] + [VMEM] * (len(operands) - 1),
+        in_specs=[VMEM] * len(operands),
         out_specs=[VMEM] * len(out_shape),
         scratch_shapes=[
             pltpu.VMEM((score_rows, 2 * rows), BF16),
@@ -258,20 +282,16 @@
             pltpu.VMEM((2 * rows, 2 * half), BF16),
         ],
         compiler_params=pltpu.CompilerParams(vmem_limit_bytes=28 << 20),
-        cost_estimate=pl.CostEstimate(
-            flops=4 * score_rows * 2 * rows * 2 * half, bytes_accessed=4 << 20, transcendentals=0
-        ),
+        cost_estimate=LOW_COST,
     )(*operands)
 
 
 def shards(spectra, wedge_ids, tilt_limits, term_freqs):
     terms, lanes = spectra.shape
     half = lanes // 2
-    padded = sum(CUTS)
     starts = [sum(CUTS[:index]) for index in range(len(CUTS))]
     group, block = lax.axis_index("pair"), lax.axis_index("blk")
     near = near_group(group)
-    near_flag = near.astype(jnp.int32)[None]
     ids = wedge_ids[None]
     limits = tilt_limits.T
 
@@ -281,51 +301,64 @@
         out_shape=jax.ShapeDtypeStruct((CUTS[0], lanes), BF16),
         in_specs=[pl.BlockSpec((CUTS[0], lanes), lambda i: (0, 0)), VMEM, SMEM, VMEM],
         out_specs=VMEM,
+        cost_estimate=LOW_COST,
     )(spectra, ids, limits, term_freqs)
-    freqs = jnp.pad(term_freqs, ((0, 0), (0, padded - terms)))
     rest = pl.pallas_call(
-        lambda *refs: rest_mask_kernel(terms, starts, *refs),
+        functools.partial(rest_mask_kernel, terms, starts),
         out_shape=[jax.ShapeDtypeStruct((rows, lanes), BF16) for rows in CUTS[1:]],
-        in_specs=[VMEM, VMEM, SMEM, VMEM],
+        in_specs=[VMEM, VMEM, SMEM, VMEM, VMEM],
         out_specs=[VMEM] * (len(CUTS) - 1),
-    )(spectra, ids, limits, freqs)
+        cost_estimate=LOW_COST,
+    )(spectra, ids, limits, term_freqs, first_chunk)
     kept = [first_chunk, *rest]
 
-    shift = jnp.array(SHIFTS, jnp.int32)
-    turns = (
-        shift[:, 0:1] * freqs[0:1] + shift[:, 1:2] * freqs[1:2] + shift[:, 2:3] * freqs[2:3]
-    )
-    angle = turns.astype(F32) * (2.0 * math.pi / BOX)
-    trig = jnp.concatenate([jnp.cos(angle), jnp.sin(angle)], axis=0)
-
+    trig = pl.pallas_call(
+        functools.partial(phase_kernel, starts),
+        out_shape=[jax.ShapeDtypeStruct((2 * SHIFT_ROWS, rows), F32) for rows in CUTS],
+        in_specs=[VMEM, ANY],
+        out_specs=[VMEM] * len(CUTS),
+        cost_estimate=LOW_COST,
+    )(term_freqs, kept[-1])
+    kept[-1], *trig = lax.optimization_barrier((kept[-1], *trig))
     crossed = [permute(chunk, cross_source) for chunk in kept]
-    got, core = [], []
-    for own, far in zip(kept, crossed):
-        got.append(permute(jnp.where(near, own, far), swap_source))
-        core.append(permute(got[-1], core_source))
+    crossed[0], kept[-1] = lax.optimization_barrier((crossed[0], kept[-1]))
+
+    sent, got, core = [], [], []
+
+    def send(index):
+        load = jnp.where(near, kept[index], crossed[index])
+        sent.append(load)
+        got.append(permute(load, swap_source))
+        core.append(permute(load, core_source))
 
     total = None
+    last = len(CUTS) - 1
+    for index in range(last):
+        send(index)
     for index, start in enumerate(starts):
         used = min(CUTS[index], terms - start)
         total, *tiles = chunk_scores(
-            used, index == 0, index == len(starts) - 1, half, near_flag, kept[index],
-            crossed[index], got[index], core[index], trig[:, start : start + CUTS[index]], total,
+            used, index == 0, index == last, half, got[index], sent[index], core[index],
+            trig[index], total,
         )
-    local, first_tile, second_tile = tiles
-    returned = permute(local, own_back_source)
-    first_back = permute(first_tile, first_back_source)
-    second_back = permute(second_tile, second_back_source)
-
-    mine = jnp.where(near, local, returned)
-    got_tile, core_tile = mine[:, :half], mine[:, half:]
+        if index == 0:
+            crossed[last], total = lax.optimization_barrier((crossed[last], total))
+            send(last)
+    rows_tile, own_tile, core_tile = tiles
+    rows_back = permute(rows_tile, first_back_source)
+    own_back = permute(own_tile, own_back_source)
+    core_back = permute(core_tile, second_back_source)
+
+    single = jnp.where(near, own_tile, own_back)
+    own_part, core_part = rows_back[:, :half], rows_back[:, half:]
     even = block % 2 == 0
     lead = near == even
     return jnp.concatenate(
         [
-            jnp.where(lead, second_back, core_tile),
-            jnp.where(even, got_tile, first_back),
-            jnp.where(lead, core_tile, second_back),
-            jnp.where(even, first_back, got_tile),
+            jnp.where(lead, core_part, core_back),
+            jnp.where(even, single, own_part),
+            jnp.where(lead, core_back, core_part),
+            jnp.where(even, own_part, single),
         ],
         axis=1,
     )

time: 62 us -> 53.1 us (0.86)
  the two profiles are of different devices: /device:TPU:0 before, /device:TPU:10 now
where the time goes in v2:
time: 53.1 us; the launch traced here: 52.8 us
  Pallas kernels  20.6 us (39%)
  starting transfers between devices  18.3 us (34%)
  waiting for transfers between devices  12.1 us (23%)
  other arithmetic  0.89 us (2%)
  local copies, waits for them, and re-layouts  0.76 us (1%)
    ppermute x12, starting transfers between devices, permute(): return lax.ppermute(value, AXES, table)  18.3 us
    pallas_call x3, Pallas kernels, chunk_scores(): pl.pallas_call(lambda *refs: chunk_kernel(used, first, last, *refs), out_...  13.2 us
    ppermute x12, waiting for transfers between devices, permute(): return lax.ppermute(value, AXES, table)  12.1 us
    pallas_call x1, Pallas kernels, shards(): pl.pallas_call(functools.partial(rest_mask_kernel, terms, starts), out_sh...  3.13 us
    pallas_call x1, Pallas kernels, shards(): pl.pallas_call(functools.partial(phase_kernel, starts), out_shape=[jax.Sh...  2.35 us
    pallas_call x1, Pallas kernels, shards(): pl.pallas_call(first_mask_kernel, grid=(1,), out_shape=jax.ShapeDtypeStru...  1.99 us
  transfers between devices with their start and end apart: 12, of which 6 were waited for; matrix products, arithmetic and copies ran while one was open for 0% of the time, Pallas kernels for 26%

profile of v2, /device:TPU:10, one launch (start us, length us, event | category | flops | bytes accessed | tf_op | source)
XLA Modules:
  0.0 52.8 jit_solution(8523384993037047446)
XLA Ops:
  0.0 2.0 %shard_map.46.done_ref = bf16[1024,128]{1,0:T(8,128)(2,1)} custom-call(bf16[3000,128]{1,0:T(8,128)(2,1)} %spectra_ref.3, s32[1,64]{1,0:T(1,128)} %bitcast.4, s32[2,8]{1,0:T(2,128)} %bitcast.2, s32[3,3000]{1,0:T(4,128)} %freqs_ref.5), custom_call_target="tpu_custom_call" | custom-call | flops 1 | bytes 1 | tf_op jit(solution)/shard_map/pallas_call | solution.py:298
  2.0 4.4 %collective-permute-start = (bf16[1024,128]{1,0:T(8,128)(2,1)}, bf16[1024,128]{1,0:T(8,128)(2,1)S(1)}, u32[]{:S(2)}, u32[]{:S(2)}) collective-permute-start(bf16[1024,128]{1,0:T(8,128)(2,1)} %shard_map.46.done_ref), channel_id=1, source_target_pairs={{22,8},{17,9},{16,10},{19,11},{18,12},{21,13},{20,14},{23,15},{14,... | collective-permute-start | bytes 786440 | tf_op jit(solution)/shard_map/ppermute | solution.py:50
  6.4 3.1 %shard_map.47 = (bf16[1024,128]{1,0:T(8,128)(2,1)}, bf16[1024,128]{1,0:T(8,128)(2,1)}) custom-call(bf16[3000,128]{1,0:T(8,128)(2,1)} %spectra_ref.3, s32[1,64]{1,0:T(1,128)} %bitcast.5, s32[2,8]{1,0:T(2,128)} %bitcast.3, s32[3,3000]{1,0:T(4,128)} %freqs_ref.5, bf16[1024,128]{1,0:T(8,128)(2,1)} %shard_map.46.done_ref), custom_call_target="tpu_custom_call" | custom-call | flops 1 | bytes 1 | tf_op jit(solution)/shard_map/pallas_call | solution.py:306
  9.5 0.0 copy-start.3
  9.5 3.4 %collective-permute-start.6 = (bf16[1024,128]{1,0:T(8,128)(2,1)}, bf16[1024,128]{1,0:T(8,128)(2,1)S(1)}, u32[]{:S(2)}, u32[]{:S(2)}) collective-permute-start(bf16[1024,128]{1,0:T(8,128)(2,1)} %get-tuple-element.31), channel_id=1, source_target_pairs={{22,8},{17,9},{16,10},{19,11},{18,12},{21,13},{20,14},{23,15},{14,... | collective-permute-start | bytes 786440 | tf_op jit(solution)/shard_map/ppermute | solution.py:50
  12.9 2.3 %shard_map.48 = (f32[32,1024]{1,0:T(8,128)}, f32[32,1024]{1,0:T(8,128)}, f32[32,1024]{1,0:T(8,128)}) custom-call(s32[3,3000]{1,0:T(4,128)} %freqs_ref.5, bf16[1024,128]{1,0:T(8,128)(2,1)} %get-tuple-element.26._), custom_call_target="tpu_custom_call" | custom-call | flops 1 | bytes 1 | tf_op jit(solution)/shard_map/pallas_call | solution.py:315
  15.3 0.0 copy-start.4
  15.3 0.0 copy-start.5
  15.3 0.0 collective-permute-done
  15.3 0.0 copy-done.3
  15.3 0.0 copy-start.1
  15.3 0.1 collective-permute-start.2
  15.4 0.1 collective-permute-start.3
  15.5 0.7 %copy-done.4 = bf16[1024,128]{1,0:T(8,128)(2,1)S(1)} copy-done((bf16[1024,128]{1,0:T(8,128)(2,1)S(1)}, bf16[1024,128]{1,0:T(8,128)(2,1)}, u32[]{:S(2)}) %copy-start.4) | copy-done | bytes 262168
  16.2 3.4 %collective-permute-start.1 = (bf16[1024,128]{1,0:T(8,128)(2,1)S(1)}, bf16[1024,128]{1,0:T(8,128)(2,1)S(1)}, u32[]{:S(2)}, u32[]{:S(2)}) collective-permute-start(bf16[1024,128]{1,0:T(8,128)(2,1)S(1)} %copy-done.4), channel_id=1, source_target_pairs={{22,8},{17,9},{16,10},{19,11},{18,12},{21,13},{20,14},{23,15},{14,... | collective-permute-start | bytes 786440 | tf_op jit(solution)/shard_map/ppermute | solution.py:50
  19.6 2.1 %collective-permute-done.6 = bf16[1024,128]{1,0:T(8,128)(2,1)S(1)} collective-permute-done((bf16[1024,128]{1,0:T(8,128)(2,1)}, bf16[1024,128]{1,0:T(8,128)(2,1)S(1)}, u32[]{:S(2)}, u32[]{:S(2)}) %collective-permute-start.6) | collective-permute-done | bytes 262176 | tf_op jit(solution)/shard_map/ppermute | solution.py:50
  21.7 0.0 copy-done.5
  21.8 0.1 collective-permute-start.7
  21.8 0.1 collective-permute-start.8
  21.9 1.9 %collective-permute-done.2.refs_0_ = bf16[1024,128]{1,0:T(8,128)(2,1)S(1)} collective-permute-done((bf16[1024,128]{1,0:T(8,128)(2,1)S(1)}, bf16[1024,128]{1,0:T(8,128)(2,1)S(1)}, u32[]{:S(2)}, u32[]{:S(2)}) %collective-permute-start.2) | collective-permute-done | bytes 262176 | tf_op jit(solution)/shard_map/ppermute | solution.py:50
  23.8 0.0 collective-permute-done.3.refs_2_
  23.8 0.0 copy-done.1
  23.8 4.0 %shard_map.49.refs_4_ = f32[1728,128]{1,0:T(8,128)S(1)} custom-call(bf16[1024,128]{1,0:T(8,128)(2,1)S(1)} %collective-permute-done.2.refs_0_, bf16[1024,128]{1,0:T(8,128)(2,1)S(1)} %broadcast_select_fusion.2.refs_1_, bf16[1024,128]{1,0:T(8,128)(2,1)S(1)} %collective-permute-done.3.refs_2_, f32[32,1024]{1,0:T(8,128)S(1)} %copy-done.1), custom_call_target="tpu_custom_call" | custom-call | flops 1 | bytes 1 | tf_op jit(solution)/shard_map/pallas_call | solution.py:274
  27.8 0.0 copy-start.2
  27.8 0.5 collective-permute-done.1
  28.4 0.0 copy-start
  28.4 0.2 collective-permute-start.4
  28.6 1.6 %collective-permute-start.5 = (bf16[1024,128]{1,0:T(8,128)(2,1)S(1)}, bf16[1024,128]{1,0:T(8,128)(2,1)S(1)}, u32[]{:S(2)}, u32[]{:S(2)}) collective-permute-start(bf16[1024,128]{1,0:T(8,128)(2,1)S(1)} %broadcast_select_fusion.1.refs_1_), channel_id=1, source_target_pairs={{1,0},{0,1},{3,2},{2,3},{5,4},{4,5},{7,6},{6,7},{9,8},{8,9},{11,10... | collective-permute-start | bytes 786440 | tf_op jit(solution)/shard_map/ppermute | solution.py:50
  30.3 0.0 collective-permute-done.7.refs_0_
  30.3 0.0 collective-permute-done.8.refs_2_
  30.3 0.0 copy-done.2
  30.3 4.1 %shard_map.50.refs_4_ = f32[1728,128]{1,0:T(8,128)S(1)} custom-call(bf16[1024,128]{1,0:T(8,128)(2,1)S(1)} %collective-permute-done.7.refs_0_, bf16[1024,128]{1,0:T(8,128)(2,1)S(1)} %broadcast_select_fusion.refs_1_, bf16[1024,128]{1,0:T(8,128)(2,1)S(1)} %collective-permute-done.8.refs_2_, f32[32,1024]{1,0:T(8,128)S(1)} %copy-done.2, ...), custom_call_target="tpu_custom_call" | custom-call | flops 1 | bytes 1 | tf_op jit(solution)/shard_map/pallas_call | solution.py:274
  34.3 2.5 %collective-permute-done.4.refs_0_ = bf16[1024,128]{1,0:T(8,128)(2,1)S(1)} collective-permute-done((bf16[1024,128]{1,0:T(8,128)(2,1)S(1)}, bf16[1024,128]{1,0:T(8,128)(2,1)S(1)}, u32[]{:S(2)}, u32[]{:S(2)}) %collective-permute-start.4) | collective-permute-done | bytes 262176 | tf_op jit(solution)/shard_map/ppermute | solution.py:50
  36.8 0.0 collective-permute-done.5.refs_2_
  36.8 0.0 copy-done
  36.8 5.1 %shard_map.51 = (f32[1728,128]{1,0:T(8,128)}, f32[64,128]{1,0:T(8,128)S(1)}, f32[64,64]{1,0:T(8,128)S(1)}, f32[64,64]{1,0:T(8,128)S(1)}) custom-call(bf16[1024,128]{1,0:T(8,128)(2,1)S(1)} %collective-permute-done.4.refs_0_, bf16[1024,128]{1,0:T(8,128)(2,1)S(1)} %broadcast_select_fusion.1.refs_1_, bf16[1024,128]{1,0:T(8,128)(2,1)S(1)} %collective-permute-done.5.refs_2_, ...), custom_call_target="tpu_custom_call" | custom-call | flops 1 | bytes 1 | tf_op jit(solution)/shard_map/pallas_call | solution.py:274
  41.9 0.9 %collective-permute-start.9 = (f32[64,128]{1,0:T(8,128)S(1)}, f32[64,128]{1,0:T(8,128)S(1)}, u32[]{:S(2)}, u32[]{:S(2)}) collective-permute-start(f32[64,128]{1,0:T(8,128)S(1)} %get-tuple-element.34), channel_id=1, source_target_pairs={{8,0},{11,1},{10,2},{13,3},{12,4},{15,5},{14,6},{9,7},{30,8},{27,9... | collective-permute-start | bytes 98312 | tf_op jit(solution)/shard_map/ppermute | solution.py:50
  42.8 1.6 %collective-permute-start.10 = (f32[64,64]{1,0:T(8,128)S(1)}, f32[64,64]{1,0:T(8,128)S(1)}, u32[]{:S(2)}, u32[]{:S(2)}) collective-permute-start(f32[64,64]{1,0:T(8,128)S(1)} %get-tuple-element.35), channel_id=1, source_target_pairs={{1,0},{0,1},{3,2},{2,3},{5,4},{4,5},{7,6},{6,7},{19,8},{16,9},{21,... | collective-permute-start | bytes 49160 | tf_op jit(solution)/shard_map/ppermute | solution.py:50
  44.4 2.5 %collective-permute-start.11 = (f32[64,64]{1,0:T(8,128)S(1)}, f32[64,64]{1,0:T(8,128)S(1)}, u32[]{:S(2)}, u32[]{:S(2)}) collective-permute-start(f32[64,64]{1,0:T(8,128)S(1)} %get-tuple-element.36), channel_id=1, source_target_pairs={{18,8},{17,9},{20,10},{19,11},{22,12},{21,13},{16,14},{23,15},{10,... | collective-permute-start | bytes 49160 | tf_op jit(solution)/shard_map/ppermute | solution.py:50
  46.9 1.2 %collective-permute-done.10 = f32[64,64]{1,0:T(8,128)S(1)} collective-permute-done((f32[64,64]{1,0:T(8,128)S(1)}, f32[64,64]{1,0:T(8,128)S(1)}, u32[]{:S(2)}, u32[]{:S(2)}) %collective-permute-start.10) | collective-permute-done | bytes 16416 | tf_op jit(solution)/shard_map/ppermute | solution.py:50
  48.1 3.9 %collective-permute-done.11 = f32[64,64]{1,0:T(8,128)S(1)} collective-permute-done((f32[64,64]{1,0:T(8,128)S(1)}, f32[64,64]{1,0:T(8,128)S(1)}, u32[]{:S(2)}, u32[]{:S(2)}) %collective-permute-start.11) | collective-permute-done | bytes 16416 | tf_op jit(solution)/shard_map/ppermute | solution.py:50
  52.0 0.0 collective-permute-done.9
  52.0 0.1 slice_select_fusion.3
  52.1 0.7 %pad_maximum_fusion = f32[64,256]{1,0:T(8,128)} fusion(f32[64,64]{1,0:T(8,128)S(1)} %get-tuple-element.41, f32[64,64]{1,0:T(8,128)S(1)} %get-tuple-element.40, f32[64,64]{1,0:T(8,128)S(1)} %get-tuple-element.42, f32[64,64]{1,0:T(8,128)S(1)} %get-tuple-element.39), kind=kLoop, calls=%fused_computation.3 | loop fusion | flops 49152 | bytes 131072 | tf_op jit(solution)/shard_map/concatenate | solution.py:356
  (3 shorter events, 0.1 us)
Async XLA Ops:
  2.0 13.3 %collective-permute-start = (bf16[1024,128]{1,0:T(8,128)(2,1)}, bf16[1024,128]{1,0:T(8,128)(2,1)S(1)}, u32[]{:S(2)}, u32[]{:S(2)}) collective-permute-start(bf16[1024,128]{1,0:T(8,128)(2,1)} %shard_map.46.done_ref), channel_id=1, source_target_pairs={{22,8},{17,9},{16,10},{19,11},{18,12},{21,13},{20,14},{23,15},{14,... | collective-permute-start | bytes 786440 | tf_op jit(solution)/shard_map/ppermute | solution.py:50
  9.5 5.8 %copy-start.3 = (bf16[1024,128]{1,0:T(8,128)(2,1)S(1)}, bf16[1024,128]{1,0:T(8,128)(2,1)}, u32[]{:S(2)}) copy-start(bf16[1024,128]{1,0:T(8,128)(2,1)} %shard_map.46.done_ref) | copy-start | bytes 786436
  9.5 12.2 %collective-permute-start.6 = (bf16[1024,128]{1,0:T(8,128)(2,1)}, bf16[1024,128]{1,0:T(8,128)(2,1)S(1)}, u32[]{:S(2)}, u32[]{:S(2)}) collective-permute-start(bf16[1024,128]{1,0:T(8,128)(2,1)} %get-tuple-element.31), channel_id=1, source_target_pairs={{22,8},{17,9},{16,10},{19,11},{18,12},{21,13},{20,14},{23,15},{14,... | collective-permute-start | bytes 786440 | tf_op jit(solution)/shard_map/ppermute | solution.py:50
  15.3 0.9 %copy-start.4 = (bf16[1024,128]{1,0:T(8,128)(2,1)S(1)}, bf16[1024,128]{1,0:T(8,128)(2,1)}, u32[]{:S(2)}) copy-start(bf16[1024,128]{1,0:T(8,128)(2,1)} %get-tuple-element.26._) | copy-start | bytes 786436
  15.3 6.4 %copy-start.5 = (bf16[1024,128]{1,0:T(8,128)(2,1)S(1)}, bf16[1024,128]{1,0:T(8,128)(2,1)}, u32[]{:S(2)}) copy-start(bf16[1024,128]{1,0:T(8,128)(2,1)} %get-tuple-element.31) | copy-start | bytes 786436
  15.3 8.4 %copy-start.1 = (f32[32,1024]{1,0:T(8,128)S(1)}, f32[32,1024]{1,0:T(8,128)}, u32[]{:S(2)}) copy-start(f32[32,1024]{1,0:T(8,128)} %get-tuple-element.28.refs_3_) | copy-start | bytes 393220
  15.3 8.4 %collective-permute-start.2 = (bf16[1024,128]{1,0:T(8,128)(2,1)S(1)}, bf16[1024,128]{1,0:T(8,128)(2,1)S(1)}, u32[]{:S(2)}, u32[]{:S(2)}) collective-permute-start(bf16[1024,128]{1,0:T(8,128)(2,1)S(1)} %broadcast_select_fusion.2.refs_1_), channel_id=1, source_target_pairs={{12,0},{15,1},{14,2},{9,3},{8,4},{11,5},{10,6},{13,7},{0,8},{7,9},... | collective-permute-start | bytes 786440 | tf_op jit(solution)/shard_map/ppermute | solution.py:50
  15.4 8.4 %collective-permute-start.3 = (bf16[1024,128]{1,0:T(8,128)(2,1)S(1)}, bf16[1024,128]{1,0:T(8,128)(2,1)S(1)}, u32[]{:S(2)}, u32[]{:S(2)}) collective-permute-start(bf16[1024,128]{1,0:T(8,128)(2,1)S(1)} %broadcast_select_fusion.2.refs_1_), channel_id=1, source_target_pairs={{1,0},{0,1},{3,2},{2,3},{5,4},{4,5},{7,6},{6,7},{9,8},{8,9},{11,10... | collective-permute-start | bytes 786440 | tf_op jit(solution)/shard_map/ppermute | solution.py:50
  16.2 12.1 %collective-permute-start.1 = (bf16[1024,128]{1,0:T(8,128)(2,1)S(1)}, bf16[1024,128]{1,0:T(8,128)(2,1)S(1)}, u32[]{:S(2)}, u32[]{:S(2)}) collective-permute-start(bf16[1024,128]{1,0:T(8,128)(2,1)S(1)} %copy-done.4), channel_id=1, source_target_pairs={{22,8},{17,9},{16,10},{19,11},{18,12},{21,13},{20,14},{23,15},{14,... | collective-permute-start | bytes 786440 | tf_op jit(solution)/shard_map/ppermute | solution.py:50
  21.8 8.5 %collective-permute-start.7 = (bf16[1024,128]{1,0:T(8,128)(2,1)S(1)}, bf16[1024,128]{1,0:T(8,128)(2,1)S(1)}, u32[]{:S(2)}, u32[]{:S(2)}) collective-permute-start(bf16[1024,128]{1,0:T(8,128)(2,1)S(1)} %broadcast_select_fusion.refs_1_), channel_id=1, source_target_pairs={{12,0},{15,1},{14,2},{9,3},{8,4},{11,5},{10,6},{13,7},{0,8},{7,9},... | collective-permute-start | bytes 786440 | tf_op jit(solution)/shard_map/ppermute | solution.py:50
  21.8 8.4 %collective-permute-start.8 = (bf16[1024,128]{1,0:T(8,128)(2,1)S(1)}, bf16[1024,128]{1,0:T(8,128)(2,1)S(1)}, u32[]{:S(2)}, u32[]{:S(2)}) collective-permute-start(bf16[1024,128]{1,0:T(8,128)(2,1)S(1)} %broadcast_select_fusion.refs_1_), channel_id=1, source_target_pairs={{1,0},{0,1},{3,2},{2,3},{5,4},{4,5},{7,6},{6,7},{9,8},{8,9},{11,10... | collective-permute-start | bytes 786440 | tf_op jit(solution)/shard_map/ppermute | solution.py:50
  27.8 2.4 %copy-start.2 = (f32[32,1024]{1,0:T(8,128)S(1)}, f32[32,1024]{1,0:T(8,128)}, u32[]{:S(2)}) copy-start(f32[32,1024]{1,0:T(8,128)} %get-tuple-element.32.refs_3_) | copy-start | bytes 393220
  28.4 8.4 %copy-start = (f32[32,1024]{1,0:T(8,128)S(1)}, f32[32,1024]{1,0:T(8,128)}, u32[]{:S(2)}) copy-start(f32[32,1024]{1,0:T(8,128)} %get-tuple-element.30.refs_3_) | copy-start | bytes 393220
  28.4 8.4 %collective-permute-start.4 = (bf16[1024,128]{1,0:T(8,128)(2,1)S(1)}, bf16[1024,128]{1,0:T(8,128)(2,1)S(1)}, u32[]{:S(2)}, u32[]{:S(2)}) collective-permute-start(bf16[1024,128]{1,0:T(8,128)(2,1)S(1)} %broadcast_select_fusion.1.refs_1_), channel_id=1, source_target_pairs={{12,0},{15,1},{14,2},{9,3},{8,4},{11,5},{10,6},{13,7},{0,8},{7,9},... | collective-permute-start | bytes 786440 | tf_op jit(solution)/shard_map/ppermute | solution.py:50
  28.6 8.2 %collective-permute-start.5 = (bf16[1024,128]{1,0:T(8,128)(2,1)S(1)}, bf16[1024,128]{1,0:T(8,128)(2,1)S(1)}, u32[]{:S(2)}, u32[]{:S(2)}) collective-permute-start(bf16[1024,128]{1,0:T(8,128)(2,1)S(1)} %broadcast_select_fusion.1.refs_1_), channel_id=1, source_target_pairs={{1,0},{0,1},{3,2},{2,3},{5,4},{4,5},{7,6},{6,7},{9,8},{8,9},{11,10... | collective-permute-start | bytes 786440 | tf_op jit(solution)/shard_map/ppermute | solution.py:50
  41.9 10.1 %collective-permute-start.9 = (f32[64,128]{1,0:T(8,128)S(1)}, f32[64,128]{1,0:T(8,128)S(1)}, u32[]{:S(2)}, u32[]{:S(2)}) collective-permute-start(f32[64,128]{1,0:T(8,128)S(1)} %get-tuple-element.34), channel_id=1, source_target_pairs={{8,0},{11,1},{10,2},{13,3},{12,4},{15,5},{14,6},{9,7},{30,8},{27,9... | collective-permute-start | bytes 98312 | tf_op jit(solution)/shard_map/ppermute | solution.py:50
  42.8 5.3 %collective-permute-start.10 = (f32[64,64]{1,0:T(8,128)S(1)}, f32[64,64]{1,0:T(8,128)S(1)}, u32[]{:S(2)}, u32[]{:S(2)}) collective-permute-start(f32[64,64]{1,0:T(8,128)S(1)} %get-tuple-element.35), channel_id=1, source_target_pairs={{1,0},{0,1},{3,2},{2,3},{5,4},{4,5},{7,6},{6,7},{19,8},{16,9},{21,... | collective-permute-start | bytes 49160 | tf_op jit(solution)/shard_map/ppermute | solution.py:50
  44.4 7.6 %collective-permute-start.11 = (f32[64,64]{1,0:T(8,128)S(1)}, f32[64,64]{1,0:T(8,128)S(1)}, u32[]{:S(2)}, u32[]{:S(2)}) collective-permute-start(f32[64,64]{1,0:T(8,128)S(1)} %get-tuple-element.36), channel_id=1, source_target_pairs={{18,8},{17,9},{20,10},{19,11},{22,12},{21,13},{16,14},{23,15},{10,... | collective-permute-start | bytes 49160 | tf_op jit(solution)/shard_map/ppermute | solution.py:50

commit v3 on v2

--- a/solution.py
+++ b/solution.py
@@ -76,12 +76,6 @@
     if near_group(group):
         return group ^ 1, block if block % 2 == 0 else block + 2
     return group ^ ROUND, block - 2 if block % 2 == 0 else block + 2
-
-
-def second_back_source(group, block, count):
-    if near_group(group):
-        return group, block ^ 1
-    return group ^ 1 ^ ROUND, block + 3 if block % 2 == 0 else block - 1
 
 
 def chunk_freqs(freqs_ref, start, rows):
@@ -312,16 +306,15 @@
     )(spectra, ids, limits, term_freqs, first_chunk)
     kept = [first_chunk, *rest]
 
+    crossed = [permute(chunk, cross_source) for chunk in kept]
+    crossed[0], kept[-1] = lax.optimization_barrier((crossed[0], kept[-1]))
     trig = pl.pallas_call(
         functools.partial(phase_kernel, starts),
         out_shape=[jax.ShapeDtypeStruct((2 * SHIFT_ROWS, rows), F32) for rows in CUTS],
         in_specs=[VMEM, ANY],
         out_specs=[VMEM] * len(CUTS),
         cost_estimate=LOW_COST,
-    )(term_freqs, kept[-1])
-    kept[-1], *trig = lax.optimization_barrier((kept[-1], *trig))
-    crossed = [permute(chunk, cross_source) for chunk in kept]
-    crossed[0], kept[-1] = lax.optimization_barrier((crossed[0], kept[-1]))
+    )(term_freqs, crossed[0])
 
     sent, got, core = [], [], []
 
@@ -346,10 +339,11 @@
             send(last)
     rows_tile, own_tile, core_tile = tiles
     rows_back = permute(rows_tile, first_back_source)
-    own_back = permute(own_tile, own_back_source)
-    core_back = permute(core_tile, second_back_source)
-
-    single = jnp.where(near, own_tile, own_back)
+    core_back = permute(core_tile, core_source)
+    both_back = permute(jnp.concatenate([own_tile, core_back], axis=1), own_back_source)
+
+    single = jnp.where(near, own_tile, both_back[:, :half])
+    core_back = jnp.where(near, core_back, both_back[:, half:])
     own_part, core_part = rows_back[:, :half], rows_back[:, half:]
     even = block % 2 == 0
     lead = near == even

time: 53.1 us -> 51.7 us (0.974)
  the two profiles are of different devices: /device:TPU:10 before, /device:TPU:14 now
where the time goes in v3:
time: 51.7 us; the launch traced here: 51.4 us
  starting transfers between devices  20.9 us (40%)
  Pallas kernels  20.7 us (40%)
  waiting for transfers between devices  7.02 us (14%)
  local copies, waits for them, and re-layouts  1.71 us (3%)
  other arithmetic  0.98 us (2%)
    ppermute x12, starting transfers between devices, permute(): return lax.ppermute(value, AXES, table)  20.9 us
    pallas_call x3, Pallas kernels, chunk_scores(): pl.pallas_call(lambda *refs: chunk_kernel(used, first, last, *refs), out_...  13.2 us
    ppermute x12, waiting for transfers between devices, permute(): return lax.ppermute(value, AXES, table)  7.02 us
    pallas_call x1, Pallas kernels, shards(): pl.pallas_call(functools.partial(rest_mask_kernel, terms, starts), out_sh...  3.13 us
    pallas_call x1, Pallas kernels, shards(): pl.pallas_call(functools.partial(phase_kernel, starts), out_shape=[jax.Sh...  2.35 us
    pallas_call x1, Pallas kernels, shards(): pl.pallas_call(first_mask_kernel, grid=(1,), out_shape=jax.ShapeDtypeStru...  1.99 us
    unnamed x14, local copies, waits for them, and re-layouts  1.71 us
  transfers between devices with their start and end apart: 12, of which 5 were waited for; matrix products, arithmetic and copies ran while one was open for 0% of the time, Pallas kernels for 26%

profile of v3, /device:TPU:14, one launch (start us, length us, event | category | flops | bytes accessed | tf_op | source)
XLA Modules:
  0.0 51.4 jit_solution(7063088745857806777)
XLA Ops:
  0.0 2.0 %shard_map.46.done_ref = bf16[1024,128]{1,0:T(8,128)(2,1)} custom-call(bf16[3000,128]{1,0:T(8,128)(2,1)} %spectra_ref.3, s32[1,64]{1,0:T(1,128)} %bitcast.4, s32[2,8]{1,0:T(2,128)} %bitcast.2, s32[3,3000]{1,0:T(4,128)} %freqs_ref.5), custom_call_target="tpu_custom_call" | custom-call | flops 1 | bytes 1 | tf_op jit(solution)/shard_map/pallas_call | solution.py:292
  2.0 0.0 copy-start.3
  2.0 3.5 %collective-permute-start = (bf16[1024,128]{1,0:T(8,128)(2,1)}, bf16[1024,128]{1,0:T(8,128)(2,1)S(1)}, u32[]{:S(2)}, u32[]{:S(2)}) collective-permute-start(bf16[1024,128]{1,0:T(8,128)(2,1)} %shard_map.46.done_ref), channel_id=1, source_target_pairs={{22,8},{17,9},{16,10},{19,11},{18,12},{21,13},{20,14},{23,15},{14,... | collective-permute-start | bytes 786440 | tf_op jit(solution)/shard_map/ppermute | solution.py:50
  5.5 3.1 %shard_map.47 = (bf16[1024,128]{1,0:T(8,128)(2,1)}, bf16[1024,128]{1,0:T(8,128)(2,1)}) custom-call(bf16[3000,128]{1,0:T(8,128)(2,1)} %spectra_ref.3, s32[1,64]{1,0:T(1,128)} %bitcast.5, s32[2,8]{1,0:T(2,128)} %bitcast.3, s32[3,3000]{1,0:T(4,128)} %freqs_ref.5, bf16[1024,128]{1,0:T(8,128)(2,1)} %shard_map.46.done_ref), custom_call_target="tpu_custom_call" | custom-call | flops 1 | bytes 1 | tf_op jit(solution)/shard_map/pallas_call | solution.py:300
  8.6 3.3 %collective-permute-start.6 = (bf16[1024,128]{1,0:T(8,128)(2,1)}, bf16[1024,128]{1,0:T(8,128)(2,1)S(1)}, u32[]{:S(2)}, u32[]{:S(2)}) collective-permute-start(bf16[1024,128]{1,0:T(8,128)(2,1)} %get-tuple-element.23), channel_id=1, source_target_pairs={{22,8},{17,9},{16,10},{19,11},{18,12},{21,13},{20,14},{23,15},{14,... | collective-permute-start | bytes 786440 | tf_op jit(solution)/shard_map/ppermute | solution.py:50
  11.9 0.3 collective-permute-done._
  12.2 0.0 copy-start.4
  12.2 0.0 copy-done.3
  12.2 0.0 copy-start.5
  12.3 0.7 %copy-done.4 = bf16[1024,128]{1,0:T(8,128)(2,1)} copy-done((bf16[1024,128]{1,0:T(8,128)(2,1)}, bf16[1024,128]{1,0:T(8,128)(2,1)S(1)}, u32[]{:S(2)}) %copy-start.4) | copy-done | bytes 262168
  12.9 0.0 copy-start.6
  12.9 0.0 collective-permute-start.2
  12.9 0.0 collective-permute-start.3
  12.9 0.3 copy-done.5
  13.3 5.6 %collective-permute-start.1 = (bf16[1024,128]{1,0:T(8,128)(2,1)S(1)}, bf16[1024,128]{1,0:T(8,128)(2,1)S(1)}, u32[]{:S(2)}, u32[]{:S(2)}) collective-permute-start(bf16[1024,128]{1,0:T(8,128)(2,1)S(1)} %copy-done.5), channel_id=1, source_target_pairs={{22,8},{17,9},{16,10},{19,11},{18,12},{21,13},{20,14},{23,15},{14,... | collective-permute-start | bytes 786440 | tf_op jit(solution)/shard_map/ppermute | solution.py:50
  18.9 2.3 %shard_map.48 = (f32[32,1024]{1,0:T(8,128)}, f32[32,1024]{1,0:T(8,128)}, f32[32,1024]{1,0:T(8,128)}) custom-call(s32[3,3000]{1,0:T(4,128)} %freqs_ref.5, bf16[1024,128]{1,0:T(8,128)(2,1)} %copy-done.4), custom_call_target="tpu_custom_call" | custom-call | flops 1 | bytes 1 | tf_op jit(solution)/shard_map/pallas_call | solution.py:311
  21.3 0.0 copy-start.1
  21.3 0.0 collective-permute-done.6
  21.3 0.0 copy-done.6
  21.3 0.1 collective-permute-start.7
  21.4 0.1 collective-permute-start.8
  21.5 0.0 collective-permute-done.2.refs_0_
  21.5 0.0 collective-permute-done.3.refs_2_
  21.5 0.7 %copy-done.1 = f32[32,1024]{1,0:T(8,128)S(1)} copy-done((f32[32,1024]{1,0:T(8,128)S(1)}, f32[32,1024]{1,0:T(8,128)}, u32[]{:S(2)}) %copy-start.1) | copy-done | bytes 131096
  22.2 4.0 %shard_map.49.refs_4_ = f32[1728,128]{1,0:T(8,128)S(1)} custom-call(bf16[1024,128]{1,0:T(8,128)(2,1)S(1)} %collective-permute-done.2.refs_0_, bf16[1024,128]{1,0:T(8,128)(2,1)S(1)} %broadcast_select_fusion.2.refs_1_, bf16[1024,128]{1,0:T(8,128)(2,1)S(1)} %collective-permute-done.3.refs_2_, f32[32,1024]{1,0:T(8,128)S(1)} %copy-done.1), custom_call_target="tpu_custom_call" | custom-call | flops 1 | bytes 1 | tf_op jit(solution)/shard_map/pallas_call | solution.py:268
  26.2 0.0 copy-start.2
  26.2 0.1 collective-permute-done.1
  26.4 1.3 %collective-permute-start.4 = (bf16[1024,128]{1,0:T(8,128)(2,1)S(1)}, bf16[1024,128]{1,0:T(8,128)(2,1)S(1)}, u32[]{:S(2)}, u32[]{:S(2)}) collective-permute-start(bf16[1024,128]{1,0:T(8,128)(2,1)S(1)} %broadcast_select_fusion.1.refs_1_), channel_id=1, source_target_pairs={{12,0},{15,1},{14,2},{9,3},{8,4},{11,5},{10,6},{13,7},{0,8},{7,9},... | collective-permute-start | bytes 786440 | tf_op jit(solution)/shard_map/ppermute | solution.py:50
  27.7 0.9 %collective-permute-start.5 = (bf16[1024,128]{1,0:T(8,128)(2,1)S(1)}, bf16[1024,128]{1,0:T(8,128)(2,1)S(1)}, u32[]{:S(2)}, u32[]{:S(2)}) collective-permute-start(bf16[1024,128]{1,0:T(8,128)(2,1)S(1)} %broadcast_select_fusion.1.refs_1_), channel_id=1, source_target_pairs={{1,0},{0,1},{3,2},{2,3},{5,4},{4,5},{7,6},{6,7},{9,8},{8,9},{11,10... | collective-permute-start | bytes 786440 | tf_op jit(solution)/shard_map/ppermute | solution.py:50
  28.6 0.9 %collective-permute-done.7.refs_0_ = bf16[1024,128]{1,0:T(8,128)(2,1)S(1)} collective-permute-done((bf16[1024,128]{1,0:T(8,128)(2,1)S(1)}, bf16[1024,128]{1,0:T(8,128)(2,1)S(1)}, u32[]{:S(2)}, u32[]{:S(2)}) %collective-permute-start.7) | collective-permute-done | bytes 262176 | tf_op jit(solution)/shard_map/ppermute | solution.py:50
  29.5 0.0 collective-permute-done.8.refs_2_
  29.5 0.0 copy-done.2
  29.5 0.0 copy-start
  29.5 4.1 %shard_map.50.refs_4_ = f32[1728,128]{1,0:T(8,128)S(1)} custom-call(bf16[1024,128]{1,0:T(8,128)(2,1)S(1)} %collective-permute-done.7.refs_0_, bf16[1024,128]{1,0:T(8,128)(2,1)S(1)} %broadcast_select_fusion.refs_1_, bf16[1024,128]{1,0:T(8,128)(2,1)S(1)} %collective-permute-done.8.refs_2_, f32[32,1024]{1,0:T(8,128)S(1)} %copy-done.2, ...), custom_call_target="tpu_custom_call" | custom-call | flops 1 | bytes 1 | tf_op jit(solution)/shard_map/pallas_call | solution.py:268
  33.6 1.6 %collective-permute-done.4.refs_0_ = bf16[1024,128]{1,0:T(8,128)(2,1)S(1)} collective-permute-done((bf16[1024,128]{1,0:T(8,128)(2,1)S(1)}, bf16[1024,128]{1,0:T(8,128)(2,1)S(1)}, u32[]{:S(2)}, u32[]{:S(2)}) %collective-permute-start.4) | collective-permute-done | bytes 262176 | tf_op jit(solution)/shard_map/ppermute | solution.py:50
  35.2 0.0 collective-permute-done.5.refs_2_
  35.2 0.0 copy-done
  35.2 5.1 %shard_map.51 = (f32[1728,128]{1,0:T(8,128)}, f32[64,128]{1,0:T(8,128)S(1)}, f32[64,64]{1,0:T(8,128)S(1)}, f32[64,64]{1,0:T(8,128)S(1)}) custom-call(bf16[1024,128]{1,0:T(8,128)(2,1)S(1)} %collective-permute-done.4.refs_0_, bf16[1024,128]{1,0:T(8,128)(2,1)S(1)} %broadcast_select_fusion.1.refs_1_, bf16[1024,128]{1,0:T(8,128)(2,1)S(1)} %collective-permute-done.5.refs_2_, ...), custom_call_target="tpu_custom_call" | custom-call | flops 1 | bytes 1 | tf_op jit(solution)/shard_map/pallas_call | solution.py:268
  40.3 0.0 collective-permute-start.10
  40.3 2.6 %collective-permute-start.9 = (f32[64,128]{1,0:T(8,128)S(1)}, f32[64,128]{1,0:T(8,128)S(1)}, u32[]{:S(2)}, u32[]{:S(2)}) collective-permute-start(f32[64,128]{1,0:T(8,128)S(1)} %get-tuple-element.26), channel_id=1, source_target_pairs={{8,0},{11,1},{10,2},{13,3},{12,4},{15,5},{14,6},{9,7},{30,8},{27,9... | collective-permute-start | bytes 98312 | tf_op jit(solution)/shard_map/ppermute | solution.py:50
  42.9 0.0 collective-permute-done.10
  42.9 0.1 pad_maximum_fusion.1
  43.0 3.4 %collective-permute-start.11 = (f32[64,128]{1,0:T(8,128)S(1)}, f32[64,128]{1,0:T(8,128)S(1)}, u32[]{:S(2)}, u32[]{:S(2)}) collective-permute-start(f32[64,128]{1,0:T(8,128)S(1)} %pad_maximum_fusion.1), channel_id=1, source_target_pairs={{18,8},{17,9},{20,10},{19,11},{22,12},{21,13},{16,14},{23,15},{10,... | collective-permute-start | bytes 98312 | tf_op jit(solution)/shard_map/ppermute | solution.py:50
  46.4 0.0 collective-permute-done.9
  46.4 4.1 %collective-permute-done.11 = f32[64,128]{1,0:T(8,128)S(1)} collective-permute-done((f32[64,128]{1,0:T(8,128)S(1)}, f32[64,128]{1,0:T(8,128)S(1)}, u32[]{:S(2)}, u32[]{:S(2)}) %collective-permute-start.11) | collective-permute-done | bytes 32800 | tf_op jit(solution)/shard_map/ppermute | solution.py:50
  50.6 0.1 slice_select_fusion.5
  50.6 0.7 %pad_maximum_fusion = f32[64,256]{1,0:T(8,128)} fusion(f32[64,64]{1,0:T(8,128)S(1)} %get-tuple-element.33, f32[64,64]{1,0:T(8,128)S(1)} %get-tuple-element.30, f32[64,64]{1,0:T(8,128)S(1)} %get-tuple-element.34, f32[64,64]{1,0:T(8,128)S(1)} %get-tuple-element.29), kind=kLoop, calls=%fused_computation.3 | loop fusion | flops 49152 | bytes 131072 | tf_op jit(solution)/shard_map/concatenate | solution.py:350
  (3 shorter events, 0.1 us)
Async XLA Ops:
  2.0 10.2 %copy-start.3 = (bf16[1024,128]{1,0:T(8,128)(2,1)S(1)}, bf16[1024,128]{1,0:T(8,128)(2,1)}, u32[]{:S(2)}) copy-start(bf16[1024,128]{1,0:T(8,128)(2,1)} %shard_map.46.done_ref) | copy-start | bytes 786436
  2.0 10.2 %collective-permute-start = (bf16[1024,128]{1,0:T(8,128)(2,1)}, bf16[1024,128]{1,0:T(8,128)(2,1)S(1)}, u32[]{:S(2)}, u32[]{:S(2)}) collective-permute-start(bf16[1024,128]{1,0:T(8,128)(2,1)} %shard_map.46.done_ref), channel_id=1, source_target_pairs={{22,8},{17,9},{16,10},{19,11},{18,12},{21,13},{20,14},{23,15},{14,... | collective-permute-start | bytes 786440 | tf_op jit(solution)/shard_map/ppermute | solution.py:50
  8.6 12.6 %collective-permute-start.6 = (bf16[1024,128]{1,0:T(8,128)(2,1)}, bf16[1024,128]{1,0:T(8,128)(2,1)S(1)}, u32[]{:S(2)}, u32[]{:S(2)}) collective-permute-start(bf16[1024,128]{1,0:T(8,128)(2,1)} %get-tuple-element.23), channel_id=1, source_target_pairs={{22,8},{17,9},{16,10},{19,11},{18,12},{21,13},{20,14},{23,15},{14,... | collective-permute-start | bytes 786440 | tf_op jit(solution)/shard_map/ppermute | solution.py:50
  12.2 0.7 %copy-start.4 = (bf16[1024,128]{1,0:T(8,128)(2,1)}, bf16[1024,128]{1,0:T(8,128)(2,1)S(1)}, u32[]{:S(2)}) copy-start(bf16[1024,128]{1,0:T(8,128)(2,1)S(1)} %collective-permute-done._) | copy-start | bytes 786436
  12.2 1.0 %copy-start.5 = (bf16[1024,128]{1,0:T(8,128)(2,1)S(1)}, bf16[1024,128]{1,0:T(8,128)(2,1)}, u32[]{:S(2)}) copy-start(bf16[1024,128]{1,0:T(8,128)(2,1)} %get-tuple-element.18) | copy-start | bytes 786436
  12.9 8.4 %copy-start.6 = (bf16[1024,128]{1,0:T(8,128)(2,1)S(1)}, bf16[1024,128]{1,0:T(8,128)(2,1)}, u32[]{:S(2)}) copy-start(bf16[1024,128]{1,0:T(8,128)(2,1)} %get-tuple-element.23) | copy-start | bytes 786436
  12.9 8.5 %collective-permute-start.2 = (bf16[1024,128]{1,0:T(8,128)(2,1)S(1)}, bf16[1024,128]{1,0:T(8,128)(2,1)S(1)}, u32[]{:S(2)}, u32[]{:S(2)}) collective-permute-start(bf16[1024,128]{1,0:T(8,128)(2,1)S(1)} %broadcast_select_fusion.2.refs_1_), channel_id=1, source_target_pairs={{12,0},{15,1},{14,2},{9,3},{8,4},{11,5},{10,6},{13,7},{0,8},{7,9},... | collective-permute-start | bytes 786440 | tf_op jit(solution)/shard_map/ppermute | solution.py:50
  12.9 8.5 %collective-permute-start.3 = (bf16[1024,128]{1,0:T(8,128)(2,1)S(1)}, bf16[1024,128]{1,0:T(8,128)(2,1)S(1)}, u32[]{:S(2)}, u32[]{:S(2)}) collective-permute-start(bf16[1024,128]{1,0:T(8,128)(2,1)S(1)} %broadcast_select_fusion.2.refs_1_), channel_id=1, source_target_pairs={{1,0},{0,1},{3,2},{2,3},{5,4},{4,5},{7,6},{6,7},{9,8},{8,9},{11,10... | collective-permute-start | bytes 786440 | tf_op jit(solution)/shard_map/ppermute | solution.py:50
  13.3 13.1 %collective-permute-start.1 = (bf16[1024,128]{1,0:T(8,128)(2,1)S(1)}, bf16[1024,128]{1,0:T(8,128)(2,1)S(1)}, u32[]{:S(2)}, u32[]{:S(2)}) collective-permute-start(bf16[1024,128]{1,0:T(8,128)(2,1)S(1)} %copy-done.5), channel_id=1, source_target_pairs={{22,8},{17,9},{16,10},{19,11},{18,12},{21,13},{20,14},{23,15},{14,... | collective-permute-start | bytes 786440 | tf_op jit(solution)/shard_map/ppermute | solution.py:50
  21.3 0.9 %copy-start.1 = (f32[32,1024]{1,0:T(8,128)S(1)}, f32[32,1024]{1,0:T(8,128)}, u32[]{:S(2)}) copy-start(f32[32,1024]{1,0:T(8,128)} %get-tuple-element.20.refs_3_) | copy-start | bytes 393220
  21.3 8.2 %collective-permute-start.7 = (bf16[1024,128]{1,0:T(8,128)(2,1)S(1)}, bf16[1024,128]{1,0:T(8,128)(2,1)S(1)}, u32[]{:S(2)}, u32[]{:S(2)}) collective-permute-start(bf16[1024,128]{1,0:T(8,128)(2,1)S(1)} %broadcast_select_fusion.refs_1_), channel_id=1, source_target_pairs={{12,0},{15,1},{14,2},{9,3},{8,4},{11,5},{10,6},{13,7},{0,8},{7,9},... | collective-permute-start | bytes 786440 | tf_op jit(solution)/shard_map/ppermute | solution.py:50
  21.4 8.1 %collective-permute-start.8 = (bf16[1024,128]{1,0:T(8,128)(2,1)S(1)}, bf16[1024,128]{1,0:T(8,128)(2,1)S(1)}, u32[]{:S(2)}, u32[]{:S(2)}) collective-permute-start(bf16[1024,128]{1,0:T(8,128)(2,1)S(1)} %broadcast_select_fusion.refs_1_), channel_id=1, source_target_pairs={{1,0},{0,1},{3,2},{2,3},{5,4},{4,5},{7,6},{6,7},{9,8},{8,9},{11,10... | collective-permute-start | bytes 786440 | tf_op jit(solution)/shard_map/ppermute | solution.py:50
  26.2 3.3 %copy-start.2 = (f32[32,1024]{1,0:T(8,128)S(1)}, f32[32,1024]{1,0:T(8,128)}, u32[]{:S(2)}) copy-start(f32[32,1024]{1,0:T(8,128)} %get-tuple-element.24.refs_3_) | copy-start | bytes 393220
  26.4 8.8 %collective-permute-start.4 = (bf16[1024,128]{1,0:T(8,128)(2,1)S(1)}, bf16[1024,128]{1,0:T(8,128)(2,1)S(1)}, u32[]{:S(2)}, u32[]{:S(2)}) collective-permute-start(bf16[1024,128]{1,0:T(8,128)(2,1)S(1)} %broadcast_select_fusion.1.refs_1_), channel_id=1, source_target_pairs={{12,0},{15,1},{14,2},{9,3},{8,4},{11,5},{10,6},{13,7},{0,8},{7,9},... | collective-permute-start | bytes 786440 | tf_op jit(solution)/shard_map/ppermute | solution.py:50
  27.7 7.5 %collective-permute-start.5 = (bf16[1024,128]{1,0:T(8,128)(2,1)S(1)}, bf16[1024,128]{1,0:T(8,128)(2,1)S(1)}, u32[]{:S(2)}, u32[]{:S(2)}) collective-permute-start(bf16[1024,128]{1,0:T(8,128)(2,1)S(1)} %broadcast_select_fusion.1.refs_1_), channel_id=1, source_target_pairs={{1,0},{0,1},{3,2},{2,3},{5,4},{4,5},{7,6},{6,7},{9,8},{8,9},{11,10... | collective-permute-start | bytes 786440 | tf_op jit(solution)/shard_map/ppermute | solution.py:50
  29.5 5.7 %copy-start = (f32[32,1024]{1,0:T(8,128)S(1)}, f32[32,1024]{1,0:T(8,128)}, u32[]{:S(2)}) copy-start(f32[32,1024]{1,0:T(8,128)} %get-tuple-element.22.refs_3_) | copy-start | bytes 393220
  40.3 2.6 %collective-permute-start.10 = (f32[64,64]{1,0:T(8,128)S(1)}, f32[64,64]{1,0:T(8,128)S(1)}, u32[]{:S(2)}, u32[]{:S(2)}) collective-permute-start(f32[64,64]{1,0:T(8,128)S(1)} %get-tuple-element.27), channel_id=1, source_target_pairs={{1,0},{0,1},{3,2},{2,3},{5,4},{4,5},{7,6},{6,7},{9,8},{8,9},{11,10... | collective-permute-start | bytes 49160 | tf_op jit(solution)/shard_map/ppermute | solution.py:50
  40.3 6.2 %collective-permute-start.9 = (f32[64,128]{1,0:T(8,128)S(1)}, f32[64,128]{1,0:T(8,128)S(1)}, u32[]{:S(2)}, u32[]{:S(2)}) collective-permute-start(f32[64,128]{1,0:T(8,128)S(1)} %get-tuple-element.26), channel_id=1, source_target_pairs={{8,0},{11,1},{10,2},{13,3},{12,4},{15,5},{14,6},{9,7},{30,8},{27,9... | collective-permute-start | bytes 98312 | tf_op jit(solution)/shard_map/ppermute | solution.py:50
  43.0 7.6 %collective-permute-start.11 = (f32[64,128]{1,0:T(8,128)S(1)}, f32[64,128]{1,0:T(8,128)S(1)}, u32[]{:S(2)}, u32[]{:S(2)}) collective-permute-start(f32[64,128]{1,0:T(8,128)S(1)} %pad_maximum_fusion.1), channel_id=1, source_target_pairs={{18,8},{17,9},{20,10},{19,11},{22,12},{21,13},{16,14},{23,15},{10,... | collective-permute-start | bytes 98312 | tf_op jit(solution)/shard_map/ppermute | solution.py:50
